TPU v7x, 512 devices: a whole 4x4x16 slice. The times are simulated.
512 devices in a mesh: lat: 16 (over z), lev: 32 (over x, y, core).
Axes of the slice: x: 4, y: 4, z: 16, core: 2. Of those that a mesh axis runs over, the one named last changes fastest.
Arguments:
- spec_in: bfloat16 [32, 2, 32, 2560], P('lat', None, None, 'lev'), may hold values from -6 to 6
- legendre: bfloat16 [32, 2560, 2560], P('lat', 'lev'), may hold values from -0.125 to 0.125
- pattern: int32 [32, 20, 20], P('lat'), may hold values from 0 to 1, as said below
- deal_list: int32 [32], replicated, may hold values from 0 to 2559, as said below
- circle_lengths: int32 [2560], replicated, may hold values from 12 to 10256, as said below
- mixing: bfloat16 [32, 32], replicated, may hold values from -1 to 1
Outputs:
- spec_out: float32 [32, 2, 32, 2560], P('lat', None, None, 'lev')
Inputs may be any that keep to these rules, and one draw needn't show every extreme that they name: `deal_list`: distinct wavenumbers; 0 and 2559 are always among them. pattern[m, a, b] is 1 exactly when b * 128 <= 2559 - deal_list[m] and a >= (deal_list[m] * 20) // 5120, else 0. `circle_lengths`: multiples of 4; row j holds a value between 20 + 4 j - 4 (j // 2 + 2) and 20 + 4 j, and the last row exactly 20 + 4 (2559).
All inputs are finite; a program needn't handle non-finite values.
Results may differ from a plain program's by a relative error of at most 0.0026.
Values may be sent and summed in bfloat16 or wider, within the bound.
No kernel may reach another device: no remote copies, remote signals or barrier semaphores. Data moves between devices by JAX's collectives and lax.ppermute only.
A program may use at most 64 MiB of HBM per device.

v0:
```python
import math

import jax
import jax.numpy as jnp
from jax import lax
from jax.sharding import PartitionSpec as P

BLK = 128


def local(spec_in, legendre, pattern, deal_list, circle_lengths, mixing):
    lat_index = lax.axis_index("lat")
    lev_index = lax.axis_index("lev")
    lat_count = lax.axis_size("lat")
    lev_count = lax.axis_size("lev")
    slot_count, local_cols, half_lat = legendre.shape
    fields = spec_in.shape[2]
    wave_count = deal_list.shape[0]
    col_blocks = pattern.shape[2]
    local_rows = half_lat // (lat_count * lev_count)
    lon_count = 20 + 4 * (half_lat - 1)
    global_cols = lev_index * local_cols + jnp.arange(local_cols, dtype=jnp.int32)
    parity = (1 - 2 * (global_cols % 2)).astype(jnp.float32)
    chooser = (
        global_cols[None, :] // BLK == jnp.arange(col_blocks, dtype=jnp.int32)[:, None]
    ).astype(jnp.bfloat16)
    row_live = jnp.repeat(pattern, BLK, axis=1).astype(jnp.bfloat16)
    block_live = jnp.einsum("sjb,bk->skj", row_live, chooser, preferred_element_type=jnp.float32)
    masked = legendre * block_live.astype(jnp.bfloat16)
    signed = (spec_in.astype(jnp.float32) * parity).astype(jnp.bfloat16)
    stacked = jnp.stack([spec_in, signed], axis=1)
    partial_value = jnp.einsum(
        "skj,shrfk->shrfj", masked, stacked, preferred_element_type=jnp.float32
    )
    summed = lax.psum_scatter(partial_value, "lev", scatter_dimension=3, tiled=True).astype(
        jnp.bfloat16
    )
    arranged = summed.reshape(
        slot_count, 2, 2, fields // lev_count, lev_count, lat_count, local_rows
    )
    fourier = lax.all_to_all(
        lax.all_to_all(arranged, "lat", split_axis=5, concat_axis=0, tiled=True),
        "lev",
        split_axis=4,
        concat_axis=3,
        tiled=True,
    )
    fourier = fourier.reshape(wave_count, 2, 2, fields, local_rows)
    row_ids = (
        lev_index * (half_lat // lev_count)
        + lat_index * local_rows
        + jnp.arange(local_rows, dtype=jnp.int32)
    )
    synth_scale = (2.0 * wave_count) ** (-0.5)
    positions = jnp.arange(lon_count, dtype=jnp.int32)

    def row_work(inputs):
        fourier_row, row_id = inputs
        length = circle_lengths[row_id]
        phases = deal_list[:, None] * positions[None, :] % length
        angles = phases.astype(jnp.float32) * (2.0 * math.pi) / length.astype(jnp.float32)
        inside = positions[None, :] < length
        cosine_table = jnp.where(inside, jnp.cos(angles), 0.0).astype(jnp.bfloat16)
        sine_table = jnp.where(inside, jnp.sin(angles), 0.0).astype(jnp.bfloat16)
        phases_table = jnp.concatenate([cosine_table, -sine_table], axis=0)
        coeffs = jnp.transpose(fourier_row, (1, 3, 2, 0)).reshape(2 * fields, 2 * wave_count)
        grid_values = (
            jnp.dot(coeffs, phases_table, preferred_element_type=jnp.float32) * synth_scale
        ).astype(jnp.bfloat16)
        grid_levels = grid_values.reshape(2, fields, lon_count)
        mixed_sum = jnp.einsum(
            "fg,hgl->hfl", mixing, grid_levels, preferred_element_type=jnp.float32
        )
        column = (
            (grid_levels.astype(jnp.float32) + jnp.tanh(mixed_sum))
            .astype(jnp.bfloat16)
            .reshape(2 * fields, lon_count)
        )
        weight = jnp.sin(math.pi * (row_id.astype(jnp.float32) + 0.5) / (2 * half_lat)) / jnp.sqrt(
            length.astype(jnp.float32)
        )
        analysis = lax.dot_general(
            column, phases_table, (((1,), (1,)), ((), ())), preferred_element_type=jnp.float32
        )
        analysis = (analysis * weight).astype(jnp.bfloat16)
        return jnp.transpose(analysis.reshape(2, fields, 2, wave_count), (3, 0, 2, 1))

    analysed = lax.map(row_work, (jnp.moveaxis(fourier, 4, 0), row_ids))
    analysed = jnp.moveaxis(analysed, 0, 4)
    arranged = analysed.reshape(wave_count, 2, 2, fields, 1, 1, local_rows)
    returned = lax.all_to_all(
        lax.all_to_all(arranged, "lat", split_axis=0, concat_axis=5, tiled=True),
        "lev",
        split_axis=3,
        concat_axis=4,
        tiled=True,
    )
    returned = returned.reshape(slot_count, 2, 2, fields // lev_count, half_lat)
    product = jnp.einsum(
        "skj,shrfj->shrfk",
        masked,
        lax.all_gather(returned, "lev", axis=3, tiled=True),
        preferred_element_type=jnp.float32,
    )
    return product[:, 0] + parity * product[:, 1]


def solution(mesh):
    return jax.shard_map(
        local,
        mesh=mesh,
        in_specs=(
            P("lat", None, None, "lev"),
            P("lat", "lev", None),
            P("lat", None, None),
            P(),
            P(),
            P(),
        ),
        out_specs=P("lat", None, None, "lev"),
        check_vma=False,
    )
```

profile of v0, /device:TPU:1, one launch (start us, length us, event | category | flops | bytes accessed | tf_op | source)
XLA Modules:
  0.0 529.0 jit_solution(8258508697396752353)
XLA Ops:
  6.6 0.8 convert_element_type.88
  7.8 0.8 fusion.32
  9.5 2.0 copy.44
  11.5 147.4 %all-reduce.2 = bf16[2,2,2,32,2560]{4,2,1,0,3:T(2,128)(2,1)} all-reduce(f32[2,2,2,32,2560]{4,2,1,0,3:T(2,128)S(1)} %copy.44), channel_id=2, replica_groups=mesh['lat'=16,'lev'=32] {'lev'}, use_global_device_ids=true, to_apply=%region_0.1.clone | all-reduce | flops 655360 | bytes 3932160
  158.9 1.3 dynamic-slice
  160.2 1.5 dynamic-slice_convert_fusion
  161.6 2.2 reshape.108
  163.9 1.2 copy.45
  165.2 0.8 reshape.124
  166.0 14.2 %all-to-all-start = ((bf16[16,2,640]{2,1,0:T(2,128)(2,1)}), bf16[16,2,640]{2,1,0:T(2,128)(2,1)S(1)}, u32[]{:S(2)}, u32[]{:S(2)}) async-start(bf16[16,2,640]{2,1,0:T(2,128)(2,1)} %reshape.124), calls=%async_computation | async-start | bytes 81920 | tf_op jit(solution)/shard_map/all_to_all | solution.py:42
  180.2 11.6 %all-to-all-done = bf16[16,2,640]{2,1,0:T(2,128)(2,1)S(1)} async-done(((bf16[16,2,640]{2,1,0:T(2,128)(2,1)}), bf16[16,2,640]{2,1,0:T(2,128)(2,1)S(1)}, u32[]{:S(2)}, u32[]{:S(2)}) %all-to-all-start) | async-done | bytes 40992 | tf_op jit(solution)/shard_map/all_to_all | solution.py:42
  192.0 0.8 reshape.126
  192.8 10.8 %all-to-all-start.1 = ((bf16[32,2,320]{2,1,0:T(2,128)(2,1)}), bf16[32,2,320]{2,1,0:T(2,128)(2,1)S(1)}, u32[]{:S(2)}, u32[]{:S(2)}) async-start(bf16[32,2,320]{2,1,0:T(2,128)(2,1)} %reshape.126), calls=%async_computation.1 | async-start | bytes 98304 | tf_op jit(solution)/shard_map/all_to_all | solution.py:41
  203.7 7.4 %all-to-all-done.1 = bf16[32,2,320]{2,1,0:T(2,128)(2,1)S(1)} async-done(((bf16[32,2,320]{2,1,0:T(2,128)(2,1)}), bf16[32,2,320]{2,1,0:T(2,128)(2,1)S(1)}, u32[]{:S(2)}, u32[]{:S(2)}) %all-to-all-start.1) | async-done | bytes 40992 | tf_op jit(solution)/shard_map/all_to_all | solution.py:41
  211.2 0.8 bitcast_bitcast_fusion
  212.0 228.6 %while.14 = (s32[]{:T(128)}, bf16[5,32,2,2,32]{4,3,0,2,1:T(2,128)(2,1)}, bf16[5,32,2,2,32]{1,3,0,2,4:T(2,128)(2,1)}, s32[5]{0:T(128)S(1)}, s32[2560]{0:T(1024)},...) while((s32[]{:T(128)}, ...), condition=%wide.region_2.3_spmd.clone.clone, body=%wide.region_1.2_spmd.clone.clone.sunk | while | flops 228111904 | bytes 9371228 | solution.py:88
  212.0 0.6 dynamic_slice.32
  214.5 1.4 dynamic_slice.33
  218.0 0.7 iota_compare_fusion.3
  218.7 17.6 %fusion.52 = bf16[32,10256]{1,0:T(8,128)(2,1)S(1)} fusion(f32[]{:T(128)S(6)} %convert_element_type.159, pred[]{:T(512)S(6)} %lt.86, s32[]{:T(128)S(6)} %select_n.96, s32[32]{0:T(128)S(1)} %get-tuple-element.255, pred[10256]{0:T(1024)(128)(4,1)S(1)} %iota_compare_fusion.3), kind=kLoop, calls=%fused_computation.22.clone.1 | loop fusion | flops 5251072 | bytes 666777 | tf_op jit(solution)/shard_map/while/body/eval_jaxpr/neg | solution.py:65
  236.3 17.5 %select_convert_fusion.3 = bf16[32,10256]{1,0:T(8,128)(2,1)S(1)} fusion(f32[]{:T(128)S(6)} %convert_element_type.159, pred[]{:T(512)S(6)} %lt.86, s32[]{:T(128)S(6)} %select_n.96, s32[32]{0:T(128)S(1)} %get-tuple-element.255, pred[10256]{0:T(1024)(128)(4,1)S(1)} %iota_compare_fusion.3), kind=kLoop, calls=%fused_computation.17.clone.1 | loop fusion | flops 4266496 | bytes 666777 | tf_op jit(solution)/shard_map/while/body/eval_jaxpr/convert_element_type | solution.py:63
  253.7 0.8 copy_bitcast_fusion.2
  256.4 0.5 fusion.55
  257.1 0.6 constant_dynamic-update-slice_fusion.2
  257.7 0.6 dynamic_slice.32
  260.3 1.4 dynamic_slice.33
  263.7 0.7 iota_compare_fusion.3
  264.4 17.6 %fusion.52 = bf16[32,10256]{1,0:T(8,128)(2,1)S(1)} fusion(f32[]{:T(128)S(6)} %convert_element_type.159, pred[]{:T(512)S(6)} %lt.86, s32[]{:T(128)S(6)} %select_n.96, s32[32]{0:T(128)S(1)} %get-tuple-element.255, pred[10256]{0:T(1024)(128)(4,1)S(1)} %iota_compare_fusion.3), kind=kLoop, calls=%fused_computation.22.clone.1 | loop fusion | flops 5251072 | bytes 666777 | tf_op jit(solution)/shard_map/while/body/eval_jaxpr/neg | solution.py:65
  282.0 17.5 %select_convert_fusion.3 = bf16[32,10256]{1,0:T(8,128)(2,1)S(1)} fusion(f32[]{:T(128)S(6)} %convert_element_type.159, pred[]{:T(512)S(6)} %lt.86, s32[]{:T(128)S(6)} %select_n.96, s32[32]{0:T(128)S(1)} %get-tuple-element.255, pred[10256]{0:T(1024)(128)(4,1)S(1)} %iota_compare_fusion.3), kind=kLoop, calls=%fused_computation.17.clone.1 | loop fusion | flops 4266496 | bytes 666777 | tf_op jit(solution)/shard_map/while/body/eval_jaxpr/convert_element_type | solution.py:63
  299.5 0.8 copy_bitcast_fusion.2
  302.1 0.5 fusion.55
  302.8 0.6 constant_dynamic-update-slice_fusion.2
  303.4 0.6 dynamic_slice.32
  306.0 1.4 dynamic_slice.33
  309.4 0.7 iota_compare_fusion.3
  310.1 17.6 %fusion.52 = bf16[32,10256]{1,0:T(8,128)(2,1)S(1)} fusion(f32[]{:T(128)S(6)} %convert_element_type.159, pred[]{:T(512)S(6)} %lt.86, s32[]{:T(128)S(6)} %select_n.96, s32[32]{0:T(128)S(1)} %get-tuple-element.255, pred[10256]{0:T(1024)(128)(4,1)S(1)} %iota_compare_fusion.3), kind=kLoop, calls=%fused_computation.22.clone.1 | loop fusion | flops 5251072 | bytes 666777 | tf_op jit(solution)/shard_map/while/body/eval_jaxpr/neg | solution.py:65
  327.7 17.5 %select_convert_fusion.3 = bf16[32,10256]{1,0:T(8,128)(2,1)S(1)} fusion(f32[]{:T(128)S(6)} %convert_element_type.159, pred[]{:T(512)S(6)} %lt.86, s32[]{:T(128)S(6)} %select_n.96, s32[32]{0:T(128)S(1)} %get-tuple-element.255, pred[10256]{0:T(1024)(128)(4,1)S(1)} %iota_compare_fusion.3), kind=kLoop, calls=%fused_computation.17.clone.1 | loop fusion | flops 4266496 | bytes 666777 | tf_op jit(solution)/shard_map/while/body/eval_jaxpr/convert_element_type | solution.py:63
  345.2 0.8 copy_bitcast_fusion.2
  347.8 0.5 fusion.55
  348.5 0.6 constant_dynamic-update-slice_fusion.2
  349.2 0.6 dynamic_slice.32
  351.7 1.4 dynamic_slice.33
  355.1 0.7 iota_compare_fusion.3
  355.8 17.6 %fusion.52 = bf16[32,10256]{1,0:T(8,128)(2,1)S(1)} fusion(f32[]{:T(128)S(6)} %convert_element_type.159, pred[]{:T(512)S(6)} %lt.86, s32[]{:T(128)S(6)} %select_n.96, s32[32]{0:T(128)S(1)} %get-tuple-element.255, pred[10256]{0:T(1024)(128)(4,1)S(1)} %iota_compare_fusion.3), kind=kLoop, calls=%fused_computation.22.clone.1 | loop fusion | flops 5251072 | bytes 666777 | tf_op jit(solution)/shard_map/while/body/eval_jaxpr/neg | solution.py:65
  373.4 17.5 %select_convert_fusion.3 = bf16[32,10256]{1,0:T(8,128)(2,1)S(1)} fusion(f32[]{:T(128)S(6)} %convert_element_type.159, pred[]{:T(512)S(6)} %lt.86, s32[]{:T(128)S(6)} %select_n.96, s32[32]{0:T(128)S(1)} %get-tuple-element.255, pred[10256]{0:T(1024)(128)(4,1)S(1)} %iota_compare_fusion.3), kind=kLoop, calls=%fused_computation.17.clone.1 | loop fusion | flops 4266496 | bytes 666777 | tf_op jit(solution)/shard_map/while/body/eval_jaxpr/convert_element_type | solution.py:63
  390.9 0.8 copy_bitcast_fusion.2
  393.5 0.5 fusion.55
  394.2 0.6 constant_dynamic-update-slice_fusion.2
  394.9 0.6 dynamic_slice.32
  397.4 1.4 dynamic_slice.33
  400.8 0.7 iota_compare_fusion.3
  401.5 17.6 %fusion.52 = bf16[32,10256]{1,0:T(8,128)(2,1)S(1)} fusion(f32[]{:T(128)S(6)} %convert_element_type.159, pred[]{:T(512)S(6)} %lt.86, s32[]{:T(128)S(6)} %select_n.96, s32[32]{0:T(128)S(1)} %get-tuple-element.255, pred[10256]{0:T(1024)(128)(4,1)S(1)} %iota_compare_fusion.3), kind=kLoop, calls=%fused_computation.22.clone.1 | loop fusion | flops 5251072 | bytes 666777 | tf_op jit(solution)/shard_map/while/body/eval_jaxpr/neg | solution.py:65
  419.1 17.5 %select_convert_fusion.3 = bf16[32,10256]{1,0:T(8,128)(2,1)S(1)} fusion(f32[]{:T(128)S(6)} %convert_element_type.159, pred[]{:T(512)S(6)} %lt.86, s32[]{:T(128)S(6)} %select_n.96, s32[32]{0:T(128)S(1)} %get-tuple-element.255, pred[10256]{0:T(1024)(128)(4,1)S(1)} %iota_compare_fusion.3), kind=kLoop, calls=%fused_computation.17.clone.1 | loop fusion | flops 4266496 | bytes 666777 | tf_op jit(solution)/shard_map/while/body/eval_jaxpr/convert_element_type | solution.py:63
  436.6 0.8 copy_bitcast_fusion.2
  439.3 0.5 fusion.55
  440.0 0.6 constant_dynamic-update-slice_fusion.2
  440.6 1.0 bitcast_bitcast_fusion.1
  441.8 14.1 %all_to_all.54 = bf16[16,2,640]{2,1,0:T(2,128)(2,1)S(1)} all-to-all(bf16[16,2,640]{2,1,0:T(2,128)(2,1)S(1)} %reshape.128), channel_id=1, replica_groups=mesh['lat'=16,'lev'=32] {'lat'}, dimensions={0} | all-to-all | bytes 81920 | tf_op jit(solution)/shard_map/all_to_all | solution.py:92
  456.9 11.8 %all_to_all.55 = bf16[32,2,320]{2,1,0:T(2,128)(2,1)S(1)} all-to-all(bf16[32,2,320]{2,1,0:T(2,128)(2,1)S(1)} %reshape.130), channel_id=1, replica_groups=mesh['lat'=16,'lev'=32] {'lev'}, dimensions={0} | all-to-all | bytes 81920 | tf_op jit(solution)/shard_map/all_to_all | solution.py:91
  468.9 1.8 copy.52
  470.7 2.1 reshape.111
  472.8 46.8 %all-gather.2.cloned.1.call-done = bf16[2,2,2,32,2560]{4,2,1,0,3:T(2,128)(2,1)} async-done(((bf16[2,2,2,1,2560]{4,2,1,0,3:T(2,128)(2,1)}), bf16[2,2,2,32,2560]{4,2,1,0,3:T(2,128)(2,1)}) %all-gather.2.cloned.1.call-update) | async-done | bytes 1310736 | tf_op jit(solution)/shard_map/all_gather | solution.py:102
  519.6 1.9 fusion.21
  521.5 0.6 fusion.28
  (52 shorter events, 9.4 us)
Async XLA Ops:
  6.5 2.0 copy-start
  7.5 1.5 copy-start.2
  163.9 48.1 %copy-start.1 = (bf16[32,32]{1,0:T(8,128)(2,1)S(1)}, bf16[32,32]{1,0:T(8,128)(2,1)}, u32[]{:S(2)}) copy-start(bf16[32,32]{1,0:T(8,128)(2,1)} %param.13) | copy-start | bytes 6148
  163.9 48.1 %copy-start.3 = (s32[32]{0:T(128)S(1)}, s32[32]{0:T(128)}, u32[]{:S(2)}) copy-start(s32[32]{0:T(128)} %param.11) | copy-start | bytes 388
  166.0 25.7 %all-to-all-start = ((bf16[16,2,640]{2,1,0:T(2,128)(2,1)}), bf16[16,2,640]{2,1,0:T(2,128)(2,1)S(1)}, u32[]{:S(2)}, u32[]{:S(2)}) async-start(bf16[16,2,640]{2,1,0:T(2,128)(2,1)} %reshape.124), calls=%async_computation | async-start | bytes 81920 | tf_op jit(solution)/shard_map/all_to_all | solution.py:42
  192.8 18.3 %all-to-all-start.1 = ((bf16[32,2,320]{2,1,0:T(2,128)(2,1)}), bf16[32,2,320]{2,1,0:T(2,128)(2,1)S(1)}, u32[]{:S(2)}, u32[]{:S(2)}) async-start(bf16[32,2,320]{2,1,0:T(2,128)(2,1)} %reshape.126), calls=%async_computation.1 | async-start | bytes 98304 | tf_op jit(solution)/shard_map/all_to_all | solution.py:41
  203.6 316.0 %all-gather.2.cloned.1.call-start = ((), (), s32[]{:S(2)}) async-start(), calls=%async_computation.4 | async-start | bytes 1351680 | tf_op jit(solution)/shard_map/all_gather | solution.py:102
Sparse Core Ops, SparseCore 0:
  473.0 46.6 all-gather.1
where the time goes:
time: 530 us; the launch traced here: 529 us
  other arithmetic  181 us (34%)
  blocking collectives  173 us (33%)
  waiting for transfers between devices  65.7 us (12%)
  local copies, waits for them, and re-layouts  35.9 us (7%)
  starting transfers between devices  25 us (5%)
  loops' own time  24.3 us (5%)
  between operations  13.6 us (3%)
  matrix products  10.2 us (2%)
    unnamed x1, blocking collectives  147 us
    neg x5, other arithmetic, row_work(): phases_table = jnp.concatenate([cosine_table, -sine_table], axis=0)  87.9 us
    convert_element_type x5, other arithmetic, row_work(): cosine_table = jnp.where(inside, jnp.cos(angles), 0.0).astype(jnp.bfloat16)  87.3 us
    all_gather x1, waiting for transfers between devices, local(): lax.all_gather(returned, 'lev', axis=3, tiled=True)  46.8 us
    another operation x1, loops' own time, local(): analysed = lax.map(row_work, (jnp.moveaxis(fourier, 4, 0), row_ids))  24.3 us
    all_to_all x1, starting transfers between devices, local(): lax.all_to_all(arranged, 'lat', split_axis=5, concat_axis=0, tiled=True)  14.2 us
    all_to_all x1, blocking collectives, local(): lax.all_to_all(arranged, 'lat', split_axis=0, concat_axis=5, tiled=True)  14.1 us
    all_to_all x1, blocking collectives, local(): lax.all_to_all(lax.all_to_all(arranged, 'lat', split_axis=0, concat_axis=...  11.8 us
  transfers between devices with their start and end apart: 3, of which 3 were waited for; matrix products, arithmetic and copies ran while one was open for 0% of the time, Pallas kernels for 0%

commit v1 on v0

v1 whole, which is shorter than its diff:
```python
import math

import jax
import jax.numpy as jnp
from jax import lax
from jax.experimental import pallas as pl
from jax.experimental.pallas import tpu as pltpu
from jax.sharding import PartitionSpec as P

BLK = 128
F32 = jnp.float32
BF16 = jnp.bfloat16
VMEM = pl.BlockSpec(memory_space=pltpu.VMEM)
SMEM = pl.BlockSpec(memory_space=pltpu.SMEM)
NT = (((1,), (1,)), ((), ()))


def params(mib):
    return pltpu.CompilerParams(vmem_limit_bytes=mib * 1024 * 1024)


def block_mask(pattern_ref, slot, row_block, first_col, shape):
    cols = shape[0]
    low = first_col // BLK
    high = (first_col + cols - 1) // BLK
    inner = lax.broadcasted_iota(jnp.int32, shape, 0) + first_col
    return jnp.where(
        inner < (low + 1) * BLK,
        pattern_ref[slot, row_block, low],
        pattern_ref[slot, row_block, high],
    ).astype(F32).astype(BF16)


def masked_half(leg_ref, pattern_ref, slot, fifth, core, first_col):
    parts = []
    cols = leg_ref.shape[1]
    for half in range(2):
        row_block = 4 * fifth + 2 * core + half
        start = pl.multiple_of(row_block * BLK, BLK)
        values = leg_ref[slot, :, pl.ds(start, BLK)]
        parts.append(values * block_mask(pattern_ref, slot, row_block, first_col, (cols, BLK)))
    return jnp.concatenate(parts, axis=1)


def inverse_kernel(place_ref, pattern_ref, spec_ref, other_spec_ref, leg_ref, other_leg_ref, out_ref):
    lev = place_ref[1]
    core = lax.rem(lev, 2)
    slots, _, fields, cols = spec_ref.shape
    chips = out_ref.shape[0]
    fifths = out_ref.shape[1] // (16 * slots)

    def stacked(ref, slot, first_col):
        column = lax.broadcasted_iota(jnp.int32, (fields, cols), 1) + first_col
        parity = (1 - 2 * lax.rem(column, 2)).astype(F32)
        rows = []
        for part in range(2):
            values = ref[slot, part].astype(F32)
            rows.append(values.astype(BF16))
            rows.append((values * parity).astype(BF16))
        return jnp.concatenate(rows, axis=0)

    mine = lev * cols
    theirs = (lev + 1 - 2 * core) * cols
    for slot in range(slots):
        left = stacked(spec_ref, slot, mine)
        other_left = stacked(other_spec_ref, slot, theirs)
        for fifth in range(fifths):
            right = masked_half(leg_ref, pattern_ref, slot, fifth, core, mine)
            other_right = masked_half(other_leg_ref, pattern_ref, slot, fifth, core, theirs)
            value = jnp.dot(left, right, preferred_element_type=F32)
            value = value + jnp.dot(other_left, other_right, preferred_element_type=F32)
            start = (slot * fifths + fifth) * 16
            out_ref[:, start : start + 16, :] = value.T.astype(BF16).reshape(chips, 16, BLK)


def sum_kernel(in_ref, out_ref, spread):
    chips, rows, _ = in_ref.shape
    lats = out_ref.shape[0]
    groups = rows // 16
    fifths = groups // 2
    spread[...] = jnp.zeros_like(spread)
    for group in range(groups):
        piece = slice(group * 16, group * 16 + 16)
        total = in_ref[0, piece, :].astype(F32)
        for chip in range(1, chips):
            total = total + in_ref[chip, piece, :].astype(F32)
        slot, fifth = divmod(group, fifths)
        spread[pl.ds(slot * 8 + fifth, lats, stride=16), :] = total
    out_ref[...] = spread[...].astype(BF16).reshape(out_ref.shape)


def copies_kernel(in_ref, out_ref, spread):
    chips, rows, _ = out_ref.shape
    lats = in_ref.shape[0]
    groups = rows // 16
    fifths = groups // 2
    spread[...] = in_ref[...].astype(F32).reshape(spread.shape)
    for group in range(groups):
        slot, fifth = divmod(group, fifths)
        value = spread[pl.ds(slot * 8 + fifth, lats, stride=16), :].astype(BF16)
        for chip in range(chips):
            out_ref[chip, group * 16 : group * 16 + 16, :] = value


def circle(x, length):
    quarter = length * 0.25
    per = 1.0 / quarter
    turns = jnp.floor(x * per + 0.5)
    rest = x - turns * quarter
    more = jnp.floor(rest * per + 0.5)
    rest = rest - more * quarter
    turns = turns + more
    turns = turns - 4.0 * jnp.floor(turns * 0.25)
    angle = rest * ((2.0 * math.pi) / length)
    sq = angle * angle
    sine = angle * (
        1.0 + sq * (-1.0 / 6 + sq * (1.0 / 120 + sq * (-1.0 / 5040 + sq * (1.0 / 362880))))
    )
    cosine = 1.0 + sq * (
        -0.5 + sq * (1.0 / 24 + sq * (-1.0 / 720 + sq * (1.0 / 40320 + sq * (-1.0 / 3628800))))
    )
    odd = (turns == 1.0) | (turns == 3.0)
    first = jnp.where(odd, sine, cosine)
    second = jnp.where(odd, cosine, sine)
    first = jnp.where((turns == 1.0) | (turns == 2.0), -first, first)
    second = jnp.where(turns >= 2.0, -second, second)
    return first, second


def row_of(place_ref, fifth, lats, chips):
    lat, lev = place_ref[0], place_ref[1]
    return fifth * (2 * lats * chips) + lax.rem(lev, 2) * (lats * chips) + (lev // 2) * lats + lat


def table_kernel(sizes, lats, chips, half_lat, place_ref, deal_ref, lengths_ref, mixing_ref,
                 table_ref, turn_ref, weight_ref, mix_ref):
    waves = deal_ref.shape[0]
    fields = mixing_ref.shape[0]
    shape = (waves, BLK)
    sub = lax.broadcasted_iota(jnp.int32, shape, 0)
    lane = lax.broadcasted_iota(jnp.int32, shape, 1)
    lane_f = lane.astype(F32)
    wave = jnp.zeros(shape, jnp.int32)
    for slot in range(waves):
        wave = jnp.where(sub == slot, deal_ref[slot], wave)
    wave_f = wave.astype(F32)
    for pair in range(2):
        quarter = 2 * pair + (lane >= BLK // 2).astype(jnp.int32)
        turn = lax.rem(quarter * wave, 4)
        turn_ref[2 * pair] = jnp.where(turn == 0, 1.0, jnp.where(turn == 2, -1.0, 0.0))
        turn_ref[2 * pair + 1] = jnp.where(turn == 1, 1.0, jnp.where(turn == 3, -1.0, 0.0))
    size = mix_ref.shape[0]
    pick = (
        lax.rem(lax.broadcasted_iota(jnp.int32, (size, fields), 0), fields)
        == lax.broadcasted_iota(jnp.int32, (size, fields), 1)
    ).astype(F32).astype(BF16)
    tall = jnp.dot(pick, mixing_ref[...], preferred_element_type=F32).astype(BF16)
    wide = lax.dot_general(tall, pick, NT, preferred_element_type=F32)
    same = (
        lax.broadcasted_iota(jnp.int32, (size, size), 0) // fields
        == lax.broadcasted_iota(jnp.int32, (size, size), 1) // fields
    )
    mix_ref[...] = jnp.where(same, wide, 0.0).astype(BF16)
    weight_ref[...] = jnp.zeros_like(weight_ref)
    start = 0
    for fifth, blocks in enumerate(sizes):
        row = row_of(place_ref, fifth, lats, chips)
        length = lengths_ref[row]
        points = length // 4
        length_f = jnp.full(shape, length, jnp.int32).astype(F32)
        low_cos, low_sin = circle(wave_f * lane_f, length_f)
        high_cos, high_sin = circle(wave_f * lane_f * float(BLK), length_f)
        for block in range(blocks):
            a_cos = jnp.broadcast_to(high_cos[:, block : block + 1], shape)
            a_sin = jnp.broadcast_to(high_sin[:, block : block + 1], shape)
            cosine = a_cos * low_cos - a_sin * low_sin
            sine = a_sin * low_cos + a_cos * low_sin
            inside = lane + block * BLK < points
            here = slice((start + block) * BLK, (start + block + 1) * BLK)
            table_ref[0:waves, here] = jnp.where(inside, cosine, 0.0).astype(BF16)
            table_ref[waves : 2 * waves, here] = jnp.where(inside, -sine, 0.0).astype(BF16)
        start += blocks
        one = (1, BLK)
        row_f = jnp.full(one, row, jnp.int32).astype(F32) + 0.5
        _, sine = circle(row_f, jnp.full(one, 4.0 * half_lat, F32))
        weight_ref[fifth : fifth + 1, :] = sine / jnp.sqrt(length_f[0:1, :])


def grid_kernel(sizes, scale, in_ref, table_ref, turn_ref, weight_ref, mix_ref, out_ref, spread, gathered):
    waves = turn_ref.shape[1]
    lane = lax.broadcasted_iota(jnp.int32, (waves, BLK), 1)
    front = lane < BLK // 2
    spread[...] = in_ref[...].astype(F32).reshape(spread.shape)
    gathered[...] = jnp.zeros_like(gathered)
    mix = mix_ref[...]
    start = 0
    for fifth, blocks in enumerate(sizes):
        value = spread[pl.ds(fifth, waves, stride=8), :] * scale
        swapped = pltpu.roll(value, BLK // 2, axis=1)
        real = jnp.where(front, value, swapped)
        imag = jnp.where(front, swapped, value)
        tops, bottoms = [], []
        for pair in range(2):
            cosine, sine = turn_ref[2 * pair], turn_ref[2 * pair + 1]
            tops.append(cosine * real - sine * imag)
            bottoms.append(sine * real + cosine * imag)
        coeffs = jnp.concatenate(
            [jnp.concatenate(tops, axis=1), jnp.concatenate(bottoms, axis=1)], axis=0
        ).T.astype(BF16)

        total = jnp.zeros((2 * waves, 2 * BLK), F32)
        done = 0
        while done < blocks:
            take = min(4, blocks - done)
            here = slice((start + done) * BLK, (start + done + take) * BLK)
            table = table_ref[:, here]
            grid = jnp.dot(coeffs, table, preferred_element_type=F32).astype(BF16)
            mixed = jnp.dot(mix, grid, preferred_element_type=F32)
            column = (grid.astype(F32) + jnp.tanh(mixed)).astype(BF16)
            total = total + lax.dot_general(table, column, NT, preferred_element_type=F32)
            done += take
        start += blocks

        real_sum = jnp.zeros((waves, BLK), F32)
        imag_sum = jnp.zeros((waves, BLK), F32)
        for pair in range(2):
            cosine, sine = turn_ref[2 * pair], turn_ref[2 * pair + 1]
            lanes = slice(pair * BLK, (pair + 1) * BLK)
            with_cos, with_sin = total[0:waves, lanes], total[waves : 2 * waves, lanes]
            real_sum = real_sum + cosine * with_cos + sine * with_sin
            imag_sum = imag_sum + cosine * with_sin - sine * with_cos
        real_sum = real_sum + pltpu.roll(real_sum, BLK // 2, axis=1)
        imag_sum = imag_sum + pltpu.roll(imag_sum, BLK // 2, axis=1)
        result = jnp.where(front, real_sum, imag_sum) * weight_ref[fifth : fifth + 1, :]
        gathered[pl.ds(fifth, waves, stride=8), :] = result
    out_ref[...] = gathered[...].astype(BF16).reshape(out_ref.shape)


def direct_kernel(place_ref, pattern_ref, mine_ref, other_ref, leg_ref, out_ref):
    lev = place_ref[1]
    core = lax.rem(lev, 2)
    slots, cols, _ = leg_ref.shape
    fields = out_ref.shape[2]
    chips, rows, _ = mine_ref.shape
    fifths = rows // (16 * slots)
    first = lev * cols
    degree = lax.broadcasted_iota(jnp.int32, (cols, BLK), 0) + first
    parity = (1 - 2 * lax.rem(degree, 2)).astype(F32)
    for slot in range(slots):
        total = jnp.zeros((cols, BLK), F32)
        for fifth in range(fifths):
            start = (slot * fifths + fifth) * 16
            for ref, owner in ((mine_ref, core), (other_ref, 1 - core)):
                left = masked_half(leg_ref, pattern_ref, slot, fifth, owner, first)
                right = ref[:, start : start + 16, :].reshape(chips * 16, BLK)
                total = total + jnp.dot(left, right, preferred_element_type=F32)
        total = total + parity * pltpu.roll(total, BLK - fields, axis=1)
        turned = total.T
        for part in range(2):
            out_ref[slot, part] = turned[2 * part * fields : (2 * part + 1) * fields, :]


def local(spec_in, legendre, pattern, deal_list, circle_lengths, mixing):
    lats, levs = lax.axis_size("lat"), lax.axis_size("lev")
    chips = levs // 2
    slots, cols, half_lat = legendre.shape
    fields = spec_in.shape[2]
    waves = deal_list.shape[0]
    fifths = half_lat // (lats * levs)
    sizes = [
        -(-(5 + (half_lat // fifths) * (fifth + 1) - 1) // BLK) for fifth in range(fifths)
    ]
    place = jnp.stack([lax.axis_index("lat"), lax.axis_index("lev")]).astype(jnp.int32)
    pairs = [(lev, lev ^ 1) for lev in range(levs)]
    same_core = [[2 * chip + core for chip in range(chips)] for core in range(2)]
    rows = slots * fifths * 16

    other_leg = lax.ppermute(legendre, "lev", pairs)
    other_spec = lax.ppermute(spec_in, "lev", pairs)

    table, turns, weights, mix = pl.pallas_call(
        lambda *refs: table_kernel(sizes, lats, chips, half_lat, *refs),
        out_shape=(
            jax.ShapeDtypeStruct((2 * waves, sum(sizes) * BLK), BF16),
            jax.ShapeDtypeStruct((4, waves, BLK), F32),
            jax.ShapeDtypeStruct((8, BLK), F32),
            jax.ShapeDtypeStruct((8 * fields, 8 * fields), BF16),
        ),
        in_specs=[SMEM, SMEM, SMEM, VMEM],
        out_specs=(VMEM, VMEM, VMEM, VMEM),
        compiler_params=params(16),
        cost_estimate=pl.CostEstimate(flops=20_000_000, bytes_accessed=4_000_000, transcendentals=0),
        name="tables",
    )(place, deal_list, circle_lengths, mixing)

    partial_sums = pl.pallas_call(
        inverse_kernel,
        out_shape=jax.ShapeDtypeStruct((chips, rows, BLK), BF16),
        in_specs=[SMEM, SMEM, VMEM, VMEM, VMEM, VMEM],
        out_specs=VMEM,
        compiler_params=params(16),
        name="inverse",
    )(place, pattern, spec_in, other_spec, legendre, other_leg)
    parts = lax.all_to_all(
        partial_sums, "lev", 0, 0, tiled=True, axis_index_groups=same_core
    )
    fourier = pl.pallas_call(
        sum_kernel,
        out_shape=jax.ShapeDtypeStruct((lats, 16, BLK), BF16),
        in_specs=[VMEM],
        out_specs=VMEM,
        scratch_shapes=[pltpu.VMEM((lats * 16, BLK), F32)],
        compiler_params=params(16),
        name="sums",
    )(parts)
    fourier = lax.all_to_all(fourier, "lat", 0, 0, tiled=True)
    analysed = pl.pallas_call(
        lambda *refs: grid_kernel(sizes, (2.0 * waves) ** (-0.5), *refs),
        out_shape=jax.ShapeDtypeStruct((lats, 16, BLK), BF16),
        in_specs=[VMEM] * 5,
        out_specs=VMEM,
        scratch_shapes=[pltpu.VMEM((lats * 16, BLK), F32), pltpu.VMEM((lats * 16, BLK), F32)],
        compiler_params=params(24),
        name="grid_rows",
    )(fourier, table, turns, weights, mix)
    analysed = lax.all_to_all(analysed, "lat", 0, 0, tiled=True)
    copies = pl.pallas_call(
        copies_kernel,
        out_shape=jax.ShapeDtypeStruct((chips, rows, BLK), BF16),
        in_specs=[VMEM],
        out_specs=VMEM,
        scratch_shapes=[pltpu.VMEM((lats * 16, BLK), F32)],
        compiler_params=params(16),
        name="copies",
    )(analysed)
    mine = lax.all_to_all(copies, "lev", 0, 0, tiled=True, axis_index_groups=same_core)
    other = lax.ppermute(mine, "lev", pairs)
    return pl.pallas_call(
        direct_kernel,
        out_shape=jax.ShapeDtypeStruct((slots, 2, fields, cols), F32),
        in_specs=[SMEM, SMEM, VMEM, VMEM, VMEM],
        out_specs=VMEM,
        compiler_params=params(16),
        name="direct",
    )(place, pattern, mine, other, legendre)


def solution(mesh):
    return jax.shard_map(
        local,
        mesh=mesh,
        in_specs=(
            P("lat", None, None, "lev"),
            P("lat", "lev", None),
            P("lat", None, None),
            P(),
            P(),
            P(),
        ),
        out_specs=P("lat", None, None, "lev"),
        check_vma=False,
    )
```

time: 530 us -> 102 us (0.19)
  other arithmetic: 181 us -> 0.08 us
  blocking collectives: 173 us -> 42.7 us
  waiting for transfers between devices: 65.7 us -> 12.2 us
  local copies, waits for them, and re-layouts: 35.9 us -> 2.66 us
  loops' own time: 24.3 us -> 0 us
  between operations: 13.6 us -> 0.12 us
  Pallas kernels: 0 us -> 12.3 us
  matrix products: 10.2 us -> 0 us
  starting transfers between devices: 25 us -> 31.1 us
    unnamed x1 -> x0, blocking collectives: 147 us -> none
    convert_element_type x6 -> x0, other arithmetic: 88.2 us -> none  [the longest x5 87.3 us: row_work(): cosine_table = jnp.where(inside, jnp.cos(angles), 0.0).astype(jnp.bfloat16)]
    neg x5 -> x0, other arithmetic: 87.9 us -> none  [row_work(): phases_table = jnp.concatenate([cosine_table, -sine_table], axis=0)]
    all_gather x1 -> x0, waiting for transfers between devices: 46.8 us -> none  [local(): lax.all_gather(returned, 'lev', axis=3, tiled=True)]
    another operation x1 -> x0, loops' own time: 24.3 us -> none  [local(): analysed = lax.map(row_work, (jnp.moveaxis(fourier, 4, 0), row_ids))]
    ppermute x0 -> x3, starting transfers between devices: none -> 17.9 us  [the longest x1 8.78 us: local(): other_leg = lax.ppermute(legendre, 'lev', pairs)]
    all_to_all x2 -> x3, blocking collectives: 25.9 us -> 42.7 us  [the longest x1 15.2 us: local(): lax.all_to_all(partial_sums, 'lev', 0, 0, tiled=True, axis_index_groups=s...]
    pallas_call x0 -> x6, Pallas kernels: none -> 12.3 us  [the longest x1 6.1 us: local(): pl.pallas_call(lambda *refs: grid_kernel(sizes, (2.0 * waves) ** (-0.5),...]
  transfers between devices with their start and end apart: 3 -> 4, of which waited for: 3 -> 3; matrix products, arithmetic and copies ran while one was open for 0% -> 1% of each run, Pallas kernels for 0% -> 2%
where the time goes in v1:
time: 102 us; the launch traced here: 101 us
  blocking collectives  42.7 us (42%)
  starting transfers between devices  31.1 us (30%)
  Pallas kernels  12.3 us (12%)
  waiting for transfers between devices  12.2 us (12%)
  local copies, waits for them, and re-layouts  2.66 us (3%)
    all_to_all x1, blocking collectives, local(): lax.all_to_all(partial_sums, 'lev', 0, 0, tiled=True, axis_index_groups=s...  15.2 us
    all_to_all x1, blocking collectives, local(): analysed = lax.all_to_all(analysed, 'lat', 0, 0, tiled=True)  14.5 us
    all_to_all x1, starting transfers between devices, local(): fourier = lax.all_to_all(fourier, 'lat', 0, 0, tiled=True)  13.2 us
    all_to_all x1, blocking collectives, local(): lax.all_to_all(copies, 'lev', 0, 0, tiled=True, axis_index_groups=same_core)  12.9 us
    all_to_all x1, waiting for transfers between devices, local(): fourier = lax.all_to_all(fourier, 'lat', 0, 0, tiled=True)  9.88 us
    ppermute x1, starting transfers between devices, local(): other_leg = lax.ppermute(legendre, 'lev', pairs)  8.78 us
    ppermute x1, starting transfers between devices, local(): other = lax.ppermute(mine, 'lev', pairs)  7.24 us
    pallas_call x1, Pallas kernels, local(): pl.pallas_call(lambda *refs: grid_kernel(sizes, (2.0 * waves) ** (-0.5),...  6.1 us
  transfers between devices with their start and end apart: 4, of which 3 were waited for; matrix products, arithmetic and copies ran while one was open for 1% of the time, Pallas kernels for 2%

profile of v1, /device:TPU:1, one launch (start us, length us, event | category | flops | bytes accessed | tf_op | source)
XLA Modules:
  0.0 101.1 jit_solution(13781341493122961400)
XLA Ops:
  0.0 8.8 %collective-permute-start.1 = (bf16[2,80,2560]{2,1,0:T(8,128)(2,1)}, bf16[2,80,2560]{2,1,0:T(8,128)(2,1)S(1)}, u32[]{:S(2)}, u32[]{:S(2)}) collective-permute-start(bf16[2,80,2560]{2,1,0:T(8,128)(2,1)} %leg_ref.3), channel_id=1, source_target_pairs={{0,1},{1,0},{2,3},{3,2},{4,5},{5,4},{6,7},{7,6},{8,9},{9,8},{10,11... | collective-permute-start | bytes 2457608 | tf_op jit(solution)/shard_map/ppermute | solution.py:278
  8.8 1.9 %collective-permute-start = (bf16[2,2,32,80]{3,2,1,0:T(8,128)(2,1)}, bf16[2,2,32,80]{3,2,1,0:T(8,128)(2,1)S(1)}, u32[]{:S(2)}, u32[]{:S(2)}) collective-permute-start(bf16[2,2,32,80]{3,2,1,0:T(8,128)(2,1)} %spec_ref.1), channel_id=1, source_target_pairs={{0,1},{1,0},{2,3},{3,2},{4,5},{5,4},{6,7},{7,6},{8,9},{9,8},{10,11... | collective-permute-start | bytes 61448 | tf_op jit(solution)/shard_map/ppermute | solution.py:279
  10.7 0.1 pad_add_fusion.place_ref.refs_0_
  10.8 0.7 copy.8.pattern_ref
  11.5 0.6 collective-permute-done.other_spec_ref
  12.1 0.0 collective-permute-done.1.other_leg_ref
  12.1 0.0 copy-start
  12.1 1.1 %copy-done = bf16[2,80,2560]{2,1,0:T(8,128)(2,1)S(1)} copy-done((bf16[2,80,2560]{2,1,0:T(8,128)(2,1)S(1)}, bf16[2,80,2560]{2,1,0:T(8,128)(2,1)}, u32[]{:S(2)}) %copy-start) | copy-done | bytes 819224
  13.2 0.0 copy-start.2
  13.3 0.8 copy-done.2
  14.0 1.6 %inverse.1 = bf16[16,160,128]{2,1,0:T(8,128)(2,1)S(1)} custom-call(s32[2]{0:T(128)S(1)} %pad_add_fusion.place_ref.refs_0_, s32[2,20,20]{2,1,0:T(8,128)S(1)} %copy.8.pattern_ref, bf16[2,2,32,80]{3,2,1,0:T(8,128)(2,1)S(1)} %copy-done.2, bf16[2,2,32,80]{3,2,1,0:T(8,128)(2,1)S(1)} %collective-permute-done.other_spec_ref, bf16[2,80,2560]{2,1,0:T(8,128)(2,1)S(1)} %copy-done, ...), custom_call_target="tpu_custom_call" | custom-call | tf_op jit(solution)/shard_map/inverse/pallas_call | solution.py:296
  15.6 0.0 copy-start.3
  15.6 0.0 copy-start.4
  15.6 0.0 copy-start.5
  15.6 15.2 %all_to_all.20.in_ref = bf16[16,160,128]{2,1,0:T(8,128)(2,1)S(1)} all-to-all(bf16[16,160,128]{2,1,0:T(8,128)(2,1)S(1)} %inverse.1), channel_id=1, replica_groups={{0,2,4,6,8,10,12,14,16,18,20,22,24,26,28,30},{1,3,5,7,9,11,13,15,17,19,..., dimensions={0} | all-to-all | bytes 1310720 | tf_op jit(solution)/shard_map/all_to_all | solution.py:304
  30.8 0.7 sums.1
  31.6 13.2 %all-to-all-start.1 = ((bf16[16,16,128]{2,1,0:T(8,128)(2,1)}), bf16[16,16,128]{2,1,0:T(8,128)(2,1)S(1)}, u32[]{:S(2)}, u32[]{:S(2)}) async-start(bf16[16,16,128]{2,1,0:T(8,128)(2,1)} %sums.1), calls=%async_computation.1 | async-start | bytes 131072 | tf_op jit(solution)/shard_map/all_to_all | solution.py:316
  44.8 0.0 copy-done.3
  44.8 0.0 copy-done.4
  44.8 0.0 copy-done.5
  44.8 1.7 %tables.1 = (bf16[64,8320]{1,0:T(8,128)(2,1)S(1)}, f32[4,32,128]{2,1,0:T(8,128)S(1)}, f32[8,128]{1,0:T(8,128)S(1)}, bf16[256,256]{1,0:T(8,128)(2,1)S(1)}) custom-call(s32[2]{0:T(128)S(1)} %pad_add_fusion.place_ref.refs_0_, s32[32]{0:T(128)S(1)} %copy-done.5, s32[2560]{0:T(1024)S(1)} %copy-done.3, bf16[32,32]{1,0:T(8,128)(2,1)S(1)} %copy-done.4), custom_call_target="tpu_custom_call" | custom-call | flops 20000000 | bytes 4000000 | tf_op jit(solution)/shard_map/tables/pallas_call | solution.py:281
  46.5 9.9 %all-to-all-done.1.refs_0_ = bf16[16,16,128]{2,1,0:T(8,128)(2,1)S(1)} async-done(((bf16[16,16,128]{2,1,0:T(8,128)(2,1)}), bf16[16,16,128]{2,1,0:T(8,128)(2,1)S(1)}, u32[]{:S(2)}, u32[]{:S(2)}) %all-to-all-start.1) | async-done | bytes 65568 | tf_op jit(solution)/shard_map/all_to_all | solution.py:316
  56.3 6.1 %grid_rows.1 = bf16[16,16,128]{2,1,0:T(8,128)(2,1)S(1)} custom-call(bf16[16,16,128]{2,1,0:T(8,128)(2,1)S(1)} %all-to-all-done.1.refs_0_, bf16[64,8320]{1,0:T(8,128)(2,1)S(1)} %get-tuple-element.9.refs_1_, f32[4,32,128]{2,1,0:T(8,128)S(1)} %get-tuple-element.10.refs_2_, f32[8,128]{1,0:T(8,128)S(1)} %get-tuple-element.11.refs_3_, ...), custom_call_target="tpu_custom_call" | custom-call | tf_op jit(solution)/shard_map/grid_rows/pallas_call | solution.py:317
  62.4 0.0 copy-start.1
  62.5 14.5 %all_to_all.21.in_ref = bf16[16,16,128]{2,1,0:T(8,128)(2,1)S(1)} all-to-all(bf16[16,16,128]{2,1,0:T(8,128)(2,1)S(1)} %grid_rows.1), channel_id=1, replica_groups=mesh['lat'=16,'lev'=32] {'lat'}, dimensions={0} | all-to-all | bytes 131072 | tf_op jit(solution)/shard_map/all_to_all | solution.py:326
  77.0 0.1 copies.1
  77.1 12.9 %all_to_all.22.mine_ref = bf16[16,160,128]{2,1,0:T(8,128)(2,1)S(1)} all-to-all(bf16[16,160,128]{2,1,0:T(8,128)(2,1)S(1)} %copies.1), channel_id=1, replica_groups={{0,2,4,6,8,10,12,14,16,18,20,22,24,26,28,30},{1,3,5,7,9,11,13,15,17,19,..., dimensions={0} | all-to-all | bytes 1310720 | tf_op jit(solution)/shard_map/all_to_all | solution.py:336
  90.0 7.2 %collective-permute-start.2 = (bf16[16,160,128]{2,1,0:T(8,128)(2,1)S(1)}, bf16[16,160,128]{2,1,0:T(8,128)(2,1)S(1)}, u32[]{:S(2)}, u32[]{:S(2)}) collective-permute-start(bf16[16,160,128]{2,1,0:T(8,128)(2,1)S(1)} %all_to_all.22.mine_ref), channel_id=1, source_target_pairs={{0,1},{1,0},{2,3},{3,2},{4,5},{5,4},{6,7},{7,6},{8,9},{9,8},{10,11... | collective-permute-start | bytes 1966088 | tf_op jit(solution)/shard_map/ppermute | solution.py:337
  97.2 1.7 %collective-permute-done.2.other_ref = bf16[16,160,128]{2,1,0:T(8,128)(2,1)S(1)} collective-permute-done((bf16[16,160,128]{2,1,0:T(8,128)(2,1)S(1)}, bf16[16,160,128]{2,1,0:T(8,128)(2,1)S(1)}, u32[]{:S(2)}, u32[]{:S(2)}) %collective-permute-start.2) | collective-permute-done | bytes 655392 | tf_op jit(solution)/shard_map/ppermute | solution.py:337
  98.9 0.0 copy-done.1
  98.9 2.2 %direct.1 = f32[2,2,32,80]{3,2,1,0:T(8,128)} custom-call(s32[2]{0:T(128)S(1)} %pad_add_fusion.place_ref.refs_0_, s32[2,20,20]{2,1,0:T(8,128)S(1)} %copy.8.pattern_ref, bf16[16,160,128]{2,1,0:T(8,128)(2,1)S(1)} %all_to_all.22.mine_ref, bf16[16,160,128]{2,1,0:T(8,128)(2,1)S(1)} %collective-permute-done.2.other_ref, bf16[2,80,2560]{2,1,0:T(8,128)(2,1)S(1)} %copy-done.1), custom_call_target="tpu_custom_call" | custom-call | tf_op jit(solution)/shard_map/direct/pallas_call | solution.py:338
Async XLA Ops:
  0.0 12.1 %collective-permute-start.1 = (bf16[2,80,2560]{2,1,0:T(8,128)(2,1)}, bf16[2,80,2560]{2,1,0:T(8,128)(2,1)S(1)}, u32[]{:S(2)}, u32[]{:S(2)}) collective-permute-start(bf16[2,80,2560]{2,1,0:T(8,128)(2,1)} %leg_ref.3), channel_id=1, source_target_pairs={{0,1},{1,0},{2,3},{3,2},{4,5},{5,4},{6,7},{7,6},{8,9},{9,8},{10,11... | collective-permute-start | bytes 2457608 | tf_op jit(solution)/shard_map/ppermute | solution.py:278
  8.8 3.3 %collective-permute-start = (bf16[2,2,32,80]{3,2,1,0:T(8,128)(2,1)}, bf16[2,2,32,80]{3,2,1,0:T(8,128)(2,1)S(1)}, u32[]{:S(2)}, u32[]{:S(2)}) collective-permute-start(bf16[2,2,32,80]{3,2,1,0:T(8,128)(2,1)} %spec_ref.1), channel_id=1, source_target_pairs={{0,1},{1,0},{2,3},{3,2},{4,5},{5,4},{6,7},{7,6},{8,9},{9,8},{10,11... | collective-permute-start | bytes 61448 | tf_op jit(solution)/shard_map/ppermute | solution.py:279
  12.1 1.1 %copy-start = (bf16[2,80,2560]{2,1,0:T(8,128)(2,1)S(1)}, bf16[2,80,2560]{2,1,0:T(8,128)(2,1)}, u32[]{:S(2)}) copy-start(bf16[2,80,2560]{2,1,0:T(8,128)(2,1)} %leg_ref.3) | copy-start | bytes 2457604
  13.2 0.8 copy-start.2
  15.6 29.2 %copy-start.3 = (s32[2560]{0:T(1024)S(1)}, s32[2560]{0:T(1024)}, u32[]{:S(2)}) copy-start(s32[2560]{0:T(1024)} %refs_2_.1) | copy-start | bytes 30724
  15.6 29.2 %copy-start.4 = (bf16[32,32]{1,0:T(8,128)(2,1)S(1)}, bf16[32,32]{1,0:T(8,128)(2,1)}, u32[]{:S(2)}) copy-start(bf16[32,32]{1,0:T(8,128)(2,1)} %refs_3_.1) | copy-start | bytes 6148
  15.6 29.2 %copy-start.5 = (s32[32]{0:T(128)S(1)}, s32[32]{0:T(128)}, u32[]{:S(2)}) copy-start(s32[32]{0:T(128)} %refs_1_.1) | copy-start | bytes 388
  31.6 24.8 %all-to-all-start.1 = ((bf16[16,16,128]{2,1,0:T(8,128)(2,1)}), bf16[16,16,128]{2,1,0:T(8,128)(2,1)S(1)}, u32[]{:S(2)}, u32[]{:S(2)}) async-start(bf16[16,16,128]{2,1,0:T(8,128)(2,1)} %sums.1), calls=%async_computation.1 | async-start | bytes 131072 | tf_op jit(solution)/shard_map/all_to_all | solution.py:316
  62.4 36.5 %copy-start.1 = (bf16[2,80,2560]{2,1,0:T(8,128)(2,1)S(1)}, bf16[2,80,2560]{2,1,0:T(8,128)(2,1)}, u32[]{:S(2)}) copy-start(bf16[2,80,2560]{2,1,0:T(8,128)(2,1)} %leg_ref.3) | copy-start | bytes 2457604
  90.0 8.9 %collective-permute-start.2 = (bf16[16,160,128]{2,1,0:T(8,128)(2,1)S(1)}, bf16[16,160,128]{2,1,0:T(8,128)(2,1)S(1)}, u32[]{:S(2)}, u32[]{:S(2)}) collective-permute-start(bf16[16,160,128]{2,1,0:T(8,128)(2,1)S(1)} %all_to_all.22.mine_ref), channel_id=1, source_target_pairs={{0,1},{1,0},{2,3},{3,2},{4,5},{5,4},{6,7},{7,6},{8,9},{9,8},{10,11... | collective-permute-start | bytes 1966088 | tf_op jit(solution)/shard_map/ppermute | solution.py:337

commit v2 on v1

--- a/solution.py
+++ b/solution.py
@@ -8,9 +8,11 @@
 from jax.sharding import PartitionSpec as P
 
 BLK = 128
+DEGREES = 2560
 F32 = jnp.float32
 BF16 = jnp.bfloat16
 VMEM = pl.BlockSpec(memory_space=pltpu.VMEM)
+ANY = pl.BlockSpec(memory_space=pl.ANY)
 SMEM = pl.BlockSpec(memory_space=pltpu.SMEM)
 NT = (((1,), (1,)), ((), ()))
 
@@ -19,55 +21,90 @@
     return pltpu.CompilerParams(vmem_limit_bytes=mib * 1024 * 1024)
 
 
-def block_mask(pattern_ref, slot, row_block, first_col, shape):
-    cols = shape[0]
-    low = first_col // BLK
-    high = (first_col + cols - 1) // BLK
-    inner = lax.broadcasted_iota(jnp.int32, shape, 0) + first_col
-    return jnp.where(
-        inner < (low + 1) * BLK,
-        pattern_ref[slot, row_block, low],
-        pattern_ref[slot, row_block, high],
-    ).astype(F32).astype(BF16)
-
-
-def masked_half(leg_ref, pattern_ref, slot, fifth, core, first_col):
-    parts = []
-    cols = leg_ref.shape[1]
-    for half in range(2):
-        row_block = 4 * fifth + 2 * core + half
-        start = pl.multiple_of(row_block * BLK, BLK)
-        values = leg_ref[slot, :, pl.ds(start, BLK)]
-        parts.append(values * block_mask(pattern_ref, slot, row_block, first_col, (cols, BLK)))
-    return jnp.concatenate(parts, axis=1)
-
-
-def inverse_kernel(place_ref, pattern_ref, spec_ref, other_spec_ref, leg_ref, other_leg_ref, out_ref):
-    lev = place_ref[1]
+def live_degrees(wave, first_col, shape):
+    degree = lax.broadcasted_iota(jnp.int32, shape, 0) + first_col
+    return degree // BLK * BLK <= DEGREES - 1 - wave
+
+
+def mask_rows(value, wave, degrees_live, row_block, row_blocks):
+    rows_live = row_block >= wave * row_blocks // (2 * DEGREES)
+    flags = jnp.logical_and(degrees_live, rows_live)
+    return jnp.where(flags, value, jnp.zeros_like(value))
+
+
+def pack_kernel(place_ref, spec_ref, leg_ref, out_ref, spec_vmem, sems):
+    other = 1 - lax.rem(place_ref[1], 2)
+    slots, cols, half_lat = leg_ref.shape
+    fields = spec_ref.shape[2]
+    fifths = half_lat // 512
+    copies = [pltpu.make_async_copy(spec_ref, spec_vmem, sems.at[0])]
+    for slot in range(slots):
+        for block in range(2 * fifths):
+            fifth, half = divmod(block, 2)
+            start = pl.multiple_of((4 * fifth + 2 * other + half) * BLK, BLK)
+            begin = (slot * 2 * fifths + block) * cols
+            copies.append(
+                pltpu.make_async_copy(
+                    leg_ref.at[slot, :, pl.ds(start, BLK)],
+                    out_ref.at[begin : begin + cols, :],
+                    sems.at[len(copies)],
+                )
+            )
+    for copy in copies:
+        copy.start()
+    begin = slots * 2 * fifths * cols
+    out_ref[begin:, :] = jnp.zeros((slots * 2 * fields, BLK), BF16)
+    copies[0].wait()
+    for slot in range(slots):
+        for part in range(2):
+            out_ref[begin : begin + fields, 0:cols] = spec_vmem[slot, part]
+            begin += fields
+    for copy in copies[1:]:
+        copy.wait()
+
+
+def inverse_kernel(place_ref, deal_ref, spec_ref, own_ref, packed_ref, out_ref, other_ref):
+    lat, lev = place_ref[0], place_ref[1]
     core = lax.rem(lev, 2)
     slots, _, fields, cols = spec_ref.shape
     chips = out_ref.shape[0]
     fifths = out_ref.shape[1] // (16 * slots)
-
-    def stacked(ref, slot, first_col):
+    mine = lev * cols
+    theirs = (lev + 1 - 2 * core) * cols
+
+    def stacked(pieces, first_col):
         column = lax.broadcasted_iota(jnp.int32, (fields, cols), 1) + first_col
         parity = (1 - 2 * lax.rem(column, 2)).astype(F32)
         rows = []
-        for part in range(2):
-            values = ref[slot, part].astype(F32)
-            rows.append(values.astype(BF16))
-            rows.append((values * parity).astype(BF16))
+        for piece in pieces:
+            rows.append(piece)
+            rows.append((piece.astype(F32) * parity).astype(BF16))
         return jnp.concatenate(rows, axis=0)
 
-    mine = lev * cols
-    theirs = (lev + 1 - 2 * core) * cols
-    for slot in range(slots):
-        left = stacked(spec_ref, slot, mine)
-        other_left = stacked(other_spec_ref, slot, theirs)
+    spec_start = slots * 2 * fifths * cols
+    for slot in range(slots):
+        wave = deal_ref[slots * lat + slot]
+        live = live_degrees(wave, theirs, (cols, BLK))
+        left = stacked([spec_ref[slot, part] for part in range(2)], mine)
+        begin = spec_start + slot * 2 * fields
+        other_left = stacked(
+            [
+                packed_ref[begin + part * fields : begin + (part + 1) * fields, 0:cols]
+                for part in range(2)
+            ],
+            theirs,
+        )
         for fifth in range(fifths):
-            right = masked_half(leg_ref, pattern_ref, slot, fifth, core, mine)
-            other_right = masked_half(other_leg_ref, pattern_ref, slot, fifth, core, theirs)
-            value = jnp.dot(left, right, preferred_element_type=F32)
+            parts = []
+            for half in range(2):
+                begin = (slot * 2 * fifths + 2 * fifth + half) * cols
+                value = packed_ref[begin : begin + cols, :]
+                row_block = 4 * fifth + 2 * core + half
+                parts.append(mask_rows(value, wave, live, row_block, 4 * fifths))
+            other_right = jnp.concatenate(parts, axis=1)
+            here = slice(fifth * 2 * BLK, (fifth + 1) * 2 * BLK)
+            other_ref[slot, :, here] = other_right
+            value = jnp.dot(left, own_ref[slot, :, here], preferred_element_type=F32)
             value = value + jnp.dot(other_left, other_right, preferred_element_type=F32)
             start = (slot * fifths + fifth) * 16
             out_ref[:, start : start + 16, :] = value.T.astype(BF16).reshape(chips, 16, BLK)
@@ -132,8 +169,22 @@
     return fifth * (2 * lats * chips) + lax.rem(lev, 2) * (lats * chips) + (lev // 2) * lats + lat
 
 
-def table_kernel(sizes, lats, chips, half_lat, place_ref, deal_ref, lengths_ref, mixing_ref,
-                 table_ref, turn_ref, weight_ref, mix_ref):
+def table_kernel(sizes, lats, chips, half_lat, place_ref, deal_ref, lengths_ref, mixing_ref, leg_ref,
+                 table_ref, turn_ref, weight_ref, mix_ref, own_ref, sems):
+    core = lax.rem(place_ref[1], 2)
+    slots, cols, _ = leg_ref.shape
+    copies = []
+    for slot in range(slots):
+        for fifth in range(len(sizes)):
+            begin = pl.multiple_of((2 * fifth + core) * 2 * BLK, 2 * BLK)
+            copies.append(
+                pltpu.make_async_copy(
+                    leg_ref.at[slot, :, pl.ds(begin, 2 * BLK)],
+                    own_ref.at[slot, :, fifth * 2 * BLK : (fifth + 1) * 2 * BLK],
+                    sems.at[len(copies)],
+                )
+            )
+            copies[-1].start()
     waves = deal_ref.shape[0]
     fields = mixing_ref.shape[0]
     shape = (waves, BLK)
@@ -184,6 +235,18 @@
         row_f = jnp.full(one, row, jnp.int32).astype(F32) + 0.5
         _, sine = circle(row_f, jnp.full(one, 4.0 * half_lat, F32))
         weight_ref[fifth : fifth + 1, :] = sine / jnp.sqrt(length_f[0:1, :])
+    for copy in copies:
+        copy.wait()
+    for slot in range(slots):
+        number = deal_ref[slots * place_ref[0] + slot]
+        live = live_degrees(number, place_ref[1] * cols, (cols, BLK))
+        for fifth in range(len(sizes)):
+            for half in range(2):
+                here = slice((2 * fifth + half) * BLK, (2 * fifth + half + 1) * BLK)
+                row_block = 4 * fifth + 2 * core + half
+                own_ref[slot, :, here] = mask_rows(
+                    own_ref[slot, :, here], number, live, row_block, 4 * len(sizes)
+                )
 
 
 def grid_kernel(sizes, scale, in_ref, table_ref, turn_ref, weight_ref, mix_ref, out_ref, spread, gathered):
@@ -236,24 +299,22 @@
     out_ref[...] = gathered[...].astype(BF16).reshape(out_ref.shape)
 
 
-def direct_kernel(place_ref, pattern_ref, mine_ref, other_ref, leg_ref, out_ref):
+def direct_kernel(mine, place_ref, rows_ref, live_ref, out_ref):
     lev = place_ref[1]
-    core = lax.rem(lev, 2)
-    slots, cols, _ = leg_ref.shape
+    owner = lev if mine else lev + 1 - 2 * lax.rem(lev, 2)
+    slots, cols, _ = live_ref.shape
     fields = out_ref.shape[2]
-    chips, rows, _ = mine_ref.shape
+    chips, rows, _ = rows_ref.shape
     fifths = rows // (16 * slots)
-    first = lev * cols
-    degree = lax.broadcasted_iota(jnp.int32, (cols, BLK), 0) + first
+    degree = lax.broadcasted_iota(jnp.int32, (cols, BLK), 0) + owner * cols
     parity = (1 - 2 * lax.rem(degree, 2)).astype(F32)
     for slot in range(slots):
         total = jnp.zeros((cols, BLK), F32)
         for fifth in range(fifths):
             start = (slot * fifths + fifth) * 16
-            for ref, owner in ((mine_ref, core), (other_ref, 1 - core)):
-                left = masked_half(leg_ref, pattern_ref, slot, fifth, owner, first)
-                right = ref[:, start : start + 16, :].reshape(chips * 16, BLK)
-                total = total + jnp.dot(left, right, preferred_element_type=F32)
+            right = rows_ref[:, start : start + 16, :].reshape(chips * 16, BLK)
+            left = live_ref[slot, :, fifth * 2 * BLK : (fifth + 1) * 2 * BLK]
+            total = total + jnp.dot(left, right, preferred_element_type=F32)
         total = total + parity * pltpu.roll(total, BLK - fields, axis=1)
         turned = total.T
         for part in range(2):
@@ -275,32 +336,48 @@
     same_core = [[2 * chip + core for chip in range(chips)] for core in range(2)]
     rows = slots * fifths * 16
 
-    other_leg = lax.ppermute(legendre, "lev", pairs)
-    other_spec = lax.ppermute(spec_in, "lev", pairs)
-
-    table, turns, weights, mix = pl.pallas_call(
+    packed = pl.pallas_call(
+        pack_kernel,
+        out_shape=jax.ShapeDtypeStruct((slots * (2 * fifths * cols + 2 * fields), BLK), BF16),
+        in_specs=[SMEM, ANY, ANY],
+        out_specs=VMEM,
+        scratch_shapes=[
+            pltpu.VMEM(spec_in.shape, BF16),
+            pltpu.SemaphoreType.DMA((1 + slots * 2 * fifths,)),
+        ],
+        compiler_params=params(16),
+        name="pack",
+    )(place, spec_in, legendre)
+    packed = lax.ppermute(packed, "lev", pairs)
+
+    table, turns, weights, mix, own = pl.pallas_call(
         lambda *refs: table_kernel(sizes, lats, chips, half_lat, *refs),
         out_shape=(
             jax.ShapeDtypeStruct((2 * waves, sum(sizes) * BLK), BF16),
             jax.ShapeDtypeStruct((4, waves, BLK), F32),
             jax.ShapeDtypeStruct((8, BLK), F32),
             jax.ShapeDtypeStruct((8 * fields, 8 * fields), BF16),
+            jax.ShapeDtypeStruct((slots, cols, fifths * 2 * BLK), BF16),
         ),
-        in_specs=[SMEM, SMEM, SMEM, VMEM],
-        out_specs=(VMEM, VMEM, VMEM, VMEM),
+        in_specs=[SMEM, SMEM, SMEM, VMEM, ANY],
+        out_specs=(VMEM,) * 5,
+        scratch_shapes=[pltpu.SemaphoreType.DMA((slots * fifths,))],
         compiler_params=params(16),
         cost_estimate=pl.CostEstimate(flops=20_000_000, bytes_accessed=4_000_000, transcendentals=0),
         name="tables",
-    )(place, deal_list, circle_lengths, mixing)
-
-    partial_sums = pl.pallas_call(
+    )(place, deal_list, circle_lengths, mixing, legendre)
+
+    partial_sums, other = pl.pallas_call(
         inverse_kernel,
-        out_shape=jax.ShapeDtypeStruct((chips, rows, BLK), BF16),
-        in_specs=[SMEM, SMEM, VMEM, VMEM, VMEM, VMEM],
-        out_specs=VMEM,
+        out_shape=(
+            jax.ShapeDtypeStruct((chips, rows, BLK), BF16),
+            jax.ShapeDtypeStruct((slots, cols, fifths * 2 * BLK), BF16),
+        ),
+        in_specs=[SMEM, SMEM, VMEM, VMEM, VMEM],
+        out_specs=(VMEM, VMEM),
         compiler_params=params(16),
         name="inverse",
-    )(place, pattern, spec_in, other_spec, legendre, other_leg)
+    )(place, deal_list, spec_in, own, packed)
     parts = lax.all_to_all(
         partial_sums, "lev", 0, 0, tiled=True, axis_index_groups=same_core
     )
@@ -333,16 +410,23 @@
         compiler_params=params(16),
         name="copies",
     )(analysed)
-    mine = lax.all_to_all(copies, "lev", 0, 0, tiled=True, axis_index_groups=same_core)
-    other = lax.ppermute(mine, "lev", pairs)
-    return pl.pallas_call(
-        direct_kernel,
-        out_shape=jax.ShapeDtypeStruct((slots, 2, fields, cols), F32),
-        in_specs=[SMEM, SMEM, VMEM, VMEM, VMEM],
-        out_specs=VMEM,
-        compiler_params=params(16),
-        name="direct",
-    )(place, pattern, mine, other, legendre)
+    gathered = lax.all_to_all(copies, "lev", 0, 0, tiled=True, axis_index_groups=same_core)
+
+    def direct(mine, live):
+        return pl.pallas_call(
+            lambda *refs: direct_kernel(mine, *refs),
+            out_shape=jax.ShapeDtypeStruct((slots, 2, fields, cols), F32),
+            in_specs=[SMEM, VMEM, VMEM],
+            out_specs=VMEM,
+            compiler_params=params(16),
+            cost_estimate=pl.CostEstimate(
+                flops=100_000_000, bytes_accessed=2_000_000, transcendentals=0
+            ),
+            name="direct_own" if mine else "direct_other",
+        )(place, gathered, live)
+
+    share = lax.ppermute(direct(False, other), "lev", pairs)
+    return direct(True, own) + share
 
 
 def solution(mesh):

time: 102 us -> 98.5 us (0.966)
  blocking collectives: 42.7 us -> 67.3 us
  starting transfers between devices: 31.1 us -> 15.8 us
  waiting for transfers between devices: 12.2 us -> 0.01 us
    all_to_all x0 -> x1, blocking collectives: none -> 24.6 us  [local(): fourier = lax.all_to_all(fourier, 'lat', 0, 0, tiled=True)]
    all_to_all x1 -> x0, starting transfers between devices: 13.2 us -> none  [local(): fourier = lax.all_to_all(fourier, 'lat', 0, 0, tiled=True)]
    all_to_all x1 -> x0, waiting for transfers between devices: 9.88 us -> none  [local(): fourier = lax.all_to_all(fourier, 'lat', 0, 0, tiled=True)]
    ppermute x3 -> x2, waiting for transfers between devices: 2.28 us -> 0.01 us  [the longest x1 0.01 us: local(): packed = lax.ppermute(packed, 'lev', pairs)]
    ppermute x3 -> x2, starting transfers between devices: 17.9 us -> 15.8 us  [the longest x1 8.79 us: local(): packed = lax.ppermute(packed, 'lev', pairs)]
    unnamed x13 -> x12, local copies, waits for them, and re-layouts: 2.66 us -> 1.92 us
    pallas_call x2 -> x4, Pallas kernels: 3.75 us -> 4.01 us  [the longest x2 1.89 us: direct(): pl.pallas_call(lambda *refs: direct_kernel(mine, *refs), out_shape=jax.Sh...]
  transfers between devices with their start and end apart: 4 -> 2, of which waited for: 3 -> 0; matrix products, arithmetic and copies ran while one was open for 1% -> 0% of each run, Pallas kernels for 2% -> 3%
where the time goes in v2:
time: 98.5 us; the launch traced here: 98.1 us
  blocking collectives  67.3 us (68%)
  starting transfers between devices  15.8 us (16%)
  Pallas kernels  12.3 us (12%)
  local copies, waits for them, and re-layouts  1.92 us (2%)
    all_to_all x1, blocking collectives, local(): fourier = lax.all_to_all(fourier, 'lat', 0, 0, tiled=True)  24.6 us
    all_to_all x1, blocking collectives, local(): lax.all_to_all(partial_sums, 'lev', 0, 0, tiled=True, axis_index_groups=s...  15.3 us
    all_to_all x1, blocking collectives, local(): analysed = lax.all_to_all(analysed, 'lat', 0, 0, tiled=True)  14.4 us
    all_to_all x1, blocking collectives, local(): lax.all_to_all(copies, 'lev', 0, 0, tiled=True, axis_index_groups=same_core)  13 us
    ppermute x1, starting transfers between devices, local(): packed = lax.ppermute(packed, 'lev', pairs)  8.79 us
    ppermute x1, starting transfers between devices, local(): share = lax.ppermute(direct(False, other), 'lev', pairs)  7 us
    pallas_call x1, Pallas kernels, local(): pl.pallas_call(lambda *refs: grid_kernel(sizes, (2.0 * waves) ** (-0.5),...  6.09 us
    pallas_call x1, Pallas kernels, local(): pl.pallas_call(lambda *refs: table_kernel(sizes, lats, chips, half_lat, *...  2.07 us
  transfers between devices with their start and end apart: 2, of which 0 were waited for; matrix products, arithmetic and copies ran while one was open for 0% of the time, Pallas kernels for 3%

profile of v2, /device:TPU:1, one launch (start us, length us, event | category | flops | bytes accessed | tf_op | source)
XLA Modules:
  0.0 98.1 jit_solution(13479195591174610072)
XLA Ops:
  0.0 0.0 copy-start.5
  0.0 0.0 copy-start.3
  0.0 0.1 pad_add_fusion.refs_0_.place_ref
  0.1 0.0 copy-start
  0.1 1.1 %copy-done = bf16[2,80,2560]{2,1,0:T(8,128)(2,1)S(1)} copy-done((bf16[2,80,2560]{2,1,0:T(8,128)(2,1)S(1)}, bf16[2,80,2560]{2,1,0:T(8,128)(2,1)}, u32[]{:S(2)}) %copy-start) | copy-done | bytes 819224
  1.2 0.0 copy-start.2
  1.2 0.8 copy-done.2
  2.0 0.0 copy-start.1
  2.0 0.0 copy-start.4
  2.0 0.9 pack.1
  2.9 8.8 %collective-permute-start = (bf16[1728,128]{1,0:T(8,128)(2,1)S(1)}, bf16[1728,128]{1,0:T(8,128)(2,1)S(1)}, u32[]{:S(2)}, u32[]{:S(2)}) collective-permute-start(bf16[1728,128]{1,0:T(8,128)(2,1)S(1)} %pack.1), channel_id=1, source_target_pairs={{0,1},{1,0},{2,3},{3,2},{4,5},{5,4},{6,7},{7,6},{8,9},{9,8},{10,11... | collective-permute-start | bytes 1327112 | tf_op jit(solution)/shard_map/ppermute | solution.py:351
  11.7 0.0 copy-done.5
  11.7 0.0 copy-done.3
  11.7 0.0 copy-done.1
  11.7 0.0 copy-done.4
  11.8 2.1 %tables.1 = (bf16[64,8320]{1,0:T(8,128)(2,1)S(1)}, f32[4,32,128]{2,1,0:T(8,128)S(1)}, f32[8,128]{1,0:T(8,128)S(1)}, bf16[256,256]{1,0:T(8,128)(2,1)S(1)}, bf16[2,80,1280]{2,1,0:T(8,128)(2,1)S(1)}) custom-call(s32[2]{0:T(128)S(1)} %pad_add_fusion.refs_0_.place_ref, s32[32]{0:T(128)S(1)} %copy-done.5, s32[2560]{0:T(1024)S(1)} %copy-done.3, ...), custom_call_target="tpu_custom_call" | custom-call | flops 20000000 | bytes 4000000 | tf_op jit(solution)/shard_map/tables/pallas_call | solution.py:353
  13.8 0.0 collective-permute-done.packed_ref
  13.8 1.2 %inverse.1 = (bf16[16,160,128]{2,1,0:T(8,128)(2,1)S(1)}, bf16[2,80,1280]{2,1,0:T(8,128)(2,1)S(1)}) custom-call(s32[2]{0:T(128)S(1)} %pad_add_fusion.refs_0_.place_ref, s32[32]{0:T(128)S(1)} %copy-done.5, bf16[2,2,32,80]{3,2,1,0:T(8,128)(2,1)S(1)} %copy-done.2, bf16[2,80,1280]{2,1,0:T(8,128)(2,1)S(1)} %get-tuple-element.12.own_ref.refs_2_, ...), custom_call_target="tpu_custom_call" | custom-call | tf_op jit(solution)/shard_map/inverse/pallas_call | solution.py:370
  15.0 15.3 %all_to_all.20.in_ref = bf16[16,160,128]{2,1,0:T(8,128)(2,1)S(1)} all-to-all(bf16[16,160,128]{2,1,0:T(8,128)(2,1)S(1)} %get-tuple-element.13), channel_id=1, replica_groups={{0,2,4,6,8,10,12,14,16,18,20,22,24,26,28,30},{1,3,5,7,9,11,13,15,17,19,..., dimensions={0} | all-to-all | bytes 1310720 | tf_op jit(solution)/shard_map/all_to_all | solution.py:381
  30.3 0.1 sums.1
  30.4 24.6 %all_to_all.21.refs_0_ = bf16[16,16,128]{2,1,0:T(8,128)(2,1)S(1)} all-to-all(bf16[16,16,128]{2,1,0:T(8,128)(2,1)S(1)} %sums.1), channel_id=1, replica_groups=mesh['lat'=16,'lev'=32] {'lat'}, dimensions={0} | all-to-all | bytes 131072 | tf_op jit(solution)/shard_map/all_to_all | solution.py:393
  55.0 6.1 %grid_rows.1 = bf16[16,16,128]{2,1,0:T(8,128)(2,1)S(1)} custom-call(bf16[16,16,128]{2,1,0:T(8,128)(2,1)S(1)} %all_to_all.21.refs_0_, bf16[64,8320]{1,0:T(8,128)(2,1)S(1)} %get-tuple-element.14.refs_1_, f32[4,32,128]{2,1,0:T(8,128)S(1)} %get-tuple-element.15.refs_2_, f32[8,128]{1,0:T(8,128)S(1)} %get-tuple-element.16.refs_3_, ...), custom_call_target="tpu_custom_call" | custom-call | tf_op jit(solution)/shard_map/grid_rows/pallas_call | solution.py:394
  61.1 14.4 %all_to_all.22.in_ref = bf16[16,16,128]{2,1,0:T(8,128)(2,1)S(1)} all-to-all(bf16[16,16,128]{2,1,0:T(8,128)(2,1)S(1)} %grid_rows.1), channel_id=1, replica_groups=mesh['lat'=16,'lev'=32] {'lat'}, dimensions={0} | all-to-all | bytes 131072 | tf_op jit(solution)/shard_map/all_to_all | solution.py:403
  75.5 0.1 copies.1
  75.6 13.0 %all_to_all.23.refs_1_ = bf16[16,160,128]{2,1,0:T(8,128)(2,1)S(1)} all-to-all(bf16[16,160,128]{2,1,0:T(8,128)(2,1)S(1)} %copies.1), channel_id=1, replica_groups={{0,2,4,6,8,10,12,14,16,18,20,22,24,26,28,30},{1,3,5,7,9,11,13,15,17,19,..., dimensions={0} | all-to-all | bytes 1310720 | tf_op jit(solution)/shard_map/all_to_all | solution.py:413
  88.6 0.9 direct_other.1
  89.5 7.0 %collective-permute-start.1 = (f32[2,2,32,80]{3,2,1,0:T(8,128)S(1)}, f32[2,2,32,80]{3,2,1,0:T(8,128)S(1)}, u32[]{:S(2)}, u32[]{:S(2)}) collective-permute-start(f32[2,2,32,80]{3,2,1,0:T(8,128)S(1)} %direct_other.1), channel_id=1, source_target_pairs={{0,1},{1,0},{2,3},{3,2},{4,5},{5,4},{6,7},{7,6},{8,9},{9,8},{10,11... | collective-permute-start | bytes 122888 | tf_op jit(solution)/shard_map/ppermute | solution.py:428
  96.5 0.9 direct_own.1
  97.5 0.0 collective-permute-done.1
  97.5 0.6 add.3
Async XLA Ops:
  0.0 11.7 %copy-start.5 = (s32[32]{0:T(128)S(1)}, s32[32]{0:T(128)}, u32[]{:S(2)}) copy-start(s32[32]{0:T(128)} %deal_ref.1) | copy-start | bytes 388
  0.0 11.7 %copy-start.3 = (s32[2560]{0:T(1024)S(1)}, s32[2560]{0:T(1024)}, u32[]{:S(2)}) copy-start(s32[2560]{0:T(1024)} %refs_2_.1) | copy-start | bytes 30724
  0.1 1.1 %copy-start = (bf16[2,80,2560]{2,1,0:T(8,128)(2,1)S(1)}, bf16[2,80,2560]{2,1,0:T(8,128)(2,1)}, u32[]{:S(2)}) copy-start(bf16[2,80,2560]{2,1,0:T(8,128)(2,1)} %leg_ref.1) | copy-start | bytes 2457604
  1.2 0.8 copy-start.2
  2.0 9.8 %copy-start.1 = (bf16[2,80,2560]{2,1,0:T(8,128)(2,1)S(1)}, bf16[2,80,2560]{2,1,0:T(8,128)(2,1)}, u32[]{:S(2)}) copy-start(bf16[2,80,2560]{2,1,0:T(8,128)(2,1)} %leg_ref.1) | copy-start | bytes 2457604
  2.0 9.8 %copy-start.4 = (bf16[32,32]{1,0:T(8,128)(2,1)S(1)}, bf16[32,32]{1,0:T(8,128)(2,1)}, u32[]{:S(2)}) copy-start(bf16[32,32]{1,0:T(8,128)(2,1)} %refs_3_.1) | copy-start | bytes 6148
  2.9 10.9 %collective-permute-start = (bf16[1728,128]{1,0:T(8,128)(2,1)S(1)}, bf16[1728,128]{1,0:T(8,128)(2,1)S(1)}, u32[]{:S(2)}, u32[]{:S(2)}) collective-permute-start(bf16[1728,128]{1,0:T(8,128)(2,1)S(1)} %pack.1), channel_id=1, source_target_pairs={{0,1},{1,0},{2,3},{3,2},{4,5},{5,4},{6,7},{7,6},{8,9},{9,8},{10,11... | collective-permute-start | bytes 1327112 | tf_op jit(solution)/shard_map/ppermute | solution.py:351
  89.5 8.0 %collective-permute-start.1 = (f32[2,2,32,80]{3,2,1,0:T(8,128)S(1)}, f32[2,2,32,80]{3,2,1,0:T(8,128)S(1)}, u32[]{:S(2)}, u32[]{:S(2)}) collective-permute-start(f32[2,2,32,80]{3,2,1,0:T(8,128)S(1)} %direct_other.1), channel_id=1, source_target_pairs={{0,1},{1,0},{2,3},{3,2},{4,5},{5,4},{6,7},{7,6},{8,9},{9,8},{10,11... | collective-permute-start | bytes 122888 | tf_op jit(solution)/shard_map/ppermute | solution.py:428

commit v3 on v2

--- a/solution.py
+++ b/solution.py
@@ -9,6 +9,7 @@
 
 BLK = 128
 DEGREES = 2560
+CHIPS = 16
 F32 = jnp.float32
 BF16 = jnp.bfloat16
 VMEM = pl.BlockSpec(memory_space=pltpu.VMEM)
@@ -17,8 +18,8 @@
 NT = (((1,), (1,)), ((), ()))
 
 
-def params(mib):
-    return pltpu.CompilerParams(vmem_limit_bytes=mib * 1024 * 1024)
+def params(kib=16384):
+    return pltpu.CompilerParams(vmem_limit_bytes=kib * 1024)
 
 
 def live_degrees(wave, first_col, shape):
@@ -30,37 +31,6 @@
     rows_live = row_block >= wave * row_blocks // (2 * DEGREES)
     flags = jnp.logical_and(degrees_live, rows_live)
     return jnp.where(flags, value, jnp.zeros_like(value))
-
-
-def pack_kernel(place_ref, spec_ref, leg_ref, out_ref, spec_vmem, sems):
-    other = 1 - lax.rem(place_ref[1], 2)
-    slots, cols, half_lat = leg_ref.shape
-    fields = spec_ref.shape[2]
-    fifths = half_lat // 512
-    copies = [pltpu.make_async_copy(spec_ref, spec_vmem, sems.at[0])]
-    for slot in range(slots):
-        for block in range(2 * fifths):
-            fifth, half = divmod(block, 2)
-            start = pl.multiple_of((4 * fifth + 2 * other + half) * BLK, BLK)
-            begin = (slot * 2 * fifths + block) * cols
-            copies.append(
-                pltpu.make_async_copy(
-                    leg_ref.at[slot, :, pl.ds(start, BLK)],
-                    out_ref.at[begin : begin + cols, :],
-                    sems.at[len(copies)],
-                )
-            )
-    for copy in copies:
-        copy.start()
-    begin = slots * 2 * fifths * cols
-    out_ref[begin:, :] = jnp.zeros((slots * 2 * fields, BLK), BF16)
-    copies[0].wait()
-    for slot in range(slots):
-        for part in range(2):
-            out_ref[begin : begin + fields, 0:cols] = spec_vmem[slot, part]
-            begin += fields
-    for copy in copies[1:]:
-        copy.wait()
 
 
 def inverse_kernel(place_ref, deal_ref, spec_ref, own_ref, packed_ref, out_ref, other_ref):
@@ -81,15 +51,14 @@
             rows.append((piece.astype(F32) * parity).astype(BF16))
         return jnp.concatenate(rows, axis=0)
 
-    spec_start = slots * 2 * fifths * cols
+    half_rows = fifths * 2 * BLK
     for slot in range(slots):
         wave = deal_ref[slots * lat + slot]
         live = live_degrees(wave, theirs, (cols, BLK))
         left = stacked([spec_ref[slot, part] for part in range(2)], mine)
-        begin = spec_start + slot * 2 * fields
         other_left = stacked(
             [
-                packed_ref[begin + part * fields : begin + (part + 1) * fields, 0:cols]
+                packed_ref[slot, part * fields : (part + 1) * fields, half_rows : half_rows + cols]
                 for part in range(2)
             ],
             theirs,
@@ -97,9 +66,9 @@
         for fifth in range(fifths):
             parts = []
             for half in range(2):
-                begin = (slot * 2 * fifths + 2 * fifth + half) * cols
-                value = packed_ref[begin : begin + cols, :]
-                row_block = 4 * fifth + 2 * core + half
+                begin = (2 * fifth + half) * BLK
+                value = packed_ref[slot, :, begin : begin + BLK]
+                row_block = 2 * fifths * core + 2 * fifth + half
                 parts.append(mask_rows(value, wave, live, row_block, 4 * fifths))
             other_right = jnp.concatenate(parts, axis=1)
             here = slice(fifth * 2 * BLK, (fifth + 1) * 2 * BLK)
@@ -164,27 +133,25 @@
     return first, second
 
 
-def row_of(place_ref, fifth, lats, chips):
+def widths(core, fifths):
+    return [2 * BLK * (core * fifths + fifth + 1) for fifth in range(fifths)]
+
+
+def table_kernel(fifths, place_ref, deal_ref, lengths_ref, mixing_ref, leg_ref,
+                 table_ref, turn_ref, weight_ref, mix_ref, gram_ref, own_ref, sems):
     lat, lev = place_ref[0], place_ref[1]
-    return fifth * (2 * lats * chips) + lax.rem(lev, 2) * (lats * chips) + (lev // 2) * lats + lat
-
-
-def table_kernel(sizes, lats, chips, half_lat, place_ref, deal_ref, lengths_ref, mixing_ref, leg_ref,
-                 table_ref, turn_ref, weight_ref, mix_ref, own_ref, sems):
-    core = lax.rem(place_ref[1], 2)
-    slots, cols, _ = leg_ref.shape
+    core = lax.rem(lev, 2)
+    slots, cols, half_lat = leg_ref.shape
+    half_rows = half_lat // 2
     copies = []
     for slot in range(slots):
-        for fifth in range(len(sizes)):
-            begin = pl.multiple_of((2 * fifth + core) * 2 * BLK, 2 * BLK)
-            copies.append(
-                pltpu.make_async_copy(
-                    leg_ref.at[slot, :, pl.ds(begin, 2 * BLK)],
-                    own_ref.at[slot, :, fifth * 2 * BLK : (fifth + 1) * 2 * BLK],
-                    sems.at[len(copies)],
-                )
+        begin = pl.multiple_of(core * half_rows, BLK)
+        copies.append(
+            pltpu.make_async_copy(
+                leg_ref.at[slot, :, pl.ds(begin, half_rows)], own_ref.at[slot], sems.at[slot]
             )
-            copies[-1].start()
+        )
+        copies[-1].start()
     waves = deal_ref.shape[0]
     fields = mixing_ref.shape[0]
     shape = (waves, BLK)
@@ -213,51 +180,85 @@
     )
     mix_ref[...] = jnp.where(same, wide, 0.0).astype(BF16)
     weight_ref[...] = jnp.zeros_like(weight_ref)
-    start = 0
-    for fifth, blocks in enumerate(sizes):
-        row = row_of(place_ref, fifth, lats, chips)
-        length = lengths_ref[row]
-        points = length // 4
-        length_f = jnp.full(shape, length, jnp.int32).astype(F32)
-        low_cos, low_sin = circle(wave_f * lane_f, length_f)
-        high_cos, high_sin = circle(wave_f * lane_f * float(BLK), length_f)
-        for block in range(blocks):
-            a_cos = jnp.broadcast_to(high_cos[:, block : block + 1], shape)
-            a_sin = jnp.broadcast_to(high_sin[:, block : block + 1], shape)
-            cosine = a_cos * low_cos - a_sin * low_sin
-            sine = a_sin * low_cos + a_cos * low_sin
-            inside = lane + block * BLK < points
-            here = slice((start + block) * BLK, (start + block + 1) * BLK)
-            table_ref[0:waves, here] = jnp.where(inside, cosine, 0.0).astype(BF16)
-            table_ref[waves : 2 * waves, here] = jnp.where(inside, -sine, 0.0).astype(BF16)
-        start += blocks
-        one = (1, BLK)
-        row_f = jnp.full(one, row, jnp.int32).astype(F32) + 0.5
-        _, sine = circle(row_f, jnp.full(one, 4.0 * half_lat, F32))
-        weight_ref[fifth : fifth + 1, :] = sine / jnp.sqrt(length_f[0:1, :])
+    group = half_rows // fifths
+    first_row = core * half_rows + (lev // 2) * (2 * BLK // CHIPS) + lat
+
+    def build(which):
+        main = widths(which, fifths)
+        extra = sum(main)
+        start = 0
+        for fifth, width in enumerate(main):
+            row = first_row + fifth * group
+            length = lengths_ref[row]
+            points = length // 4
+            length_f = jnp.full(shape, length, jnp.int32).astype(F32)
+            low_cos, low_sin = circle(wave_f * lane_f, length_f)
+            high_cos, high_sin = circle(wave_f * lane_f * float(BLK), length_f)
+            blocks = width // BLK
+            for block in range(blocks + 1):
+                a_cos = jnp.broadcast_to(high_cos[:, block : block + 1], shape)
+                a_sin = jnp.broadcast_to(high_sin[:, block : block + 1], shape)
+                cosine = a_cos * low_cos - a_sin * low_sin
+                sine = a_sin * low_cos + a_cos * low_sin
+                inside = lane + block * BLK < points
+                begin = start + block * BLK if block < blocks else extra + fifth * BLK
+                here = slice(begin, begin + BLK)
+                table_ref[0:waves, here] = jnp.where(inside, cosine, 0.0).astype(BF16)
+                table_ref[waves : 2 * waves, here] = jnp.where(inside, -sine, 0.0).astype(BF16)
+            row_f = jnp.full((1, BLK), row, jnp.int32).astype(F32) + 0.5
+            _, sine = circle(row_f, jnp.full((1, BLK), 4.0 * half_lat, F32))
+            weight_ref[fifth : fifth + 1, :] = sine / jnp.sqrt(length_f[0:1, :])
+            start += width
+        start = 0
+        for fifth, width in enumerate(main):
+            table = table_ref[:, start : start + width]
+            gram = lax.dot_general(table, table, NT, preferred_element_type=F32)
+            table = table_ref[:, extra + fifth * BLK : extra + (fifth + 1) * BLK]
+            gram = gram + lax.dot_general(table, table, NT, preferred_element_type=F32)
+            gram_ref[fifth] = two_terms(gram)
+            start += width
+
+    pl.when(core == 0)(lambda: build(0))
+    pl.when(core == 1)(lambda: build(1))
     for copy in copies:
         copy.wait()
     for slot in range(slots):
-        number = deal_ref[slots * place_ref[0] + slot]
-        live = live_degrees(number, place_ref[1] * cols, (cols, BLK))
-        for fifth in range(len(sizes)):
-            for half in range(2):
-                here = slice((2 * fifth + half) * BLK, (2 * fifth + half + 1) * BLK)
-                row_block = 4 * fifth + 2 * core + half
-                own_ref[slot, :, here] = mask_rows(
-                    own_ref[slot, :, here], number, live, row_block, 4 * len(sizes)
-                )
-
-
-def grid_kernel(sizes, scale, in_ref, table_ref, turn_ref, weight_ref, mix_ref, out_ref, spread, gathered):
+        number = deal_ref[slots * lat + slot]
+        live = live_degrees(number, lev * cols, (cols, BLK))
+        for block in range(2 * fifths):
+            here = slice(block * BLK, (block + 1) * BLK)
+            row_block = 2 * fifths * core + block
+            own_ref[slot, :, here] = mask_rows(
+                own_ref[slot, :, here], number, live, row_block, 4 * fifths
+            )
+
+
+def two_terms(value):
+    high = value.astype(BF16)
+    low = (value - high.astype(F32)).astype(BF16)
+    return jnp.concatenate([high, low], axis=1)
+
+
+def grid_kernel(scale, place_ref, lengths_ref, in_ref, table_ref, turn_ref, weight_ref, mix_ref, gram_ref,
+                out_ref, spread, gathered, totals, mixed_coeffs):
+    fifths = gram_ref.shape[0]
     waves = turn_ref.shape[1]
+    core = lax.rem(place_ref[1], 2)
     lane = lax.broadcasted_iota(jnp.int32, (waves, BLK), 1)
     front = lane < BLK // 2
     spread[...] = in_ref[...].astype(F32).reshape(spread.shape)
     gathered[...] = jnp.zeros_like(gathered)
     mix = mix_ref[...]
-    start = 0
-    for fifth, blocks in enumerate(sizes):
+    group = 2 * BLK
+    first_row = core * fifths * group + (place_ref[1] // 2) * (group // CHIPS) + place_ref[0]
+
+    def analysed(table, fifth):
+        twice = jnp.concatenate([table, table], axis=0)
+        mixed = jnp.dot(mixed_coeffs[fifth], twice, preferred_element_type=F32)
+        change = jnp.tanh(mixed).astype(BF16)
+        return lax.dot_general(table, change, NT, preferred_element_type=F32)
+
+    for fifth in range(fifths):
         value = spread[pl.ds(fifth, waves, stride=8), :] * scale
         swapped = pltpu.roll(value, BLK // 2, axis=1)
         real = jnp.where(front, value, swapped)
@@ -269,21 +270,37 @@
             bottoms.append(sine * real + cosine * imag)
         coeffs = jnp.concatenate(
             [jnp.concatenate(tops, axis=1), jnp.concatenate(bottoms, axis=1)], axis=0
-        ).T.astype(BF16)
-
-        total = jnp.zeros((2 * waves, 2 * BLK), F32)
-        done = 0
-        while done < blocks:
-            take = min(4, blocks - done)
-            here = slice((start + done) * BLK, (start + done + take) * BLK)
-            table = table_ref[:, here]
-            grid = jnp.dot(coeffs, table, preferred_element_type=F32).astype(BF16)
-            mixed = jnp.dot(mix, grid, preferred_element_type=F32)
-            column = (grid.astype(F32) + jnp.tanh(mixed)).astype(BF16)
-            total = total + lax.dot_general(table, column, NT, preferred_element_type=F32)
-            done += take
-        start += blocks
-
+        ).astype(BF16)
+        mixed_coeffs[fifth] = two_terms(
+            lax.dot_general(mix, coeffs, NT, preferred_element_type=F32)
+        )
+        totals[fifth] = jnp.dot(
+            gram_ref[fifth], jnp.concatenate([coeffs, coeffs], axis=0), preferred_element_type=F32
+        )
+
+    def rows(which):
+        main = widths(which, fifths)
+        start = 0
+        for fifth, width in enumerate(main):
+            total = totals[fifth]
+            for begin in range(start, start + width, 4 * BLK):
+                end = min(begin + 4 * BLK, start + width)
+                total = total + analysed(table_ref[:, begin:end], fifth)
+            totals[fifth] = total
+            start += width
+        for fifth, width in enumerate(main):
+            begin = start + fifth * BLK
+            points = lengths_ref[first_row + fifth * group] // 4
+
+            @pl.when(points > width)
+            def _():
+                totals[fifth] += analysed(table_ref[:, begin : begin + BLK], fifth)
+
+    pl.when(core == 0)(lambda: rows(0))
+    pl.when(core == 1)(lambda: rows(1))
+
+    for fifth in range(fifths):
+        total = totals[fifth]
         real_sum = jnp.zeros((waves, BLK), F32)
         imag_sum = jnp.zeros((waves, BLK), F32)
         for pair in range(2):
@@ -328,41 +345,38 @@
     fields = spec_in.shape[2]
     waves = deal_list.shape[0]
     fifths = half_lat // (lats * levs)
-    sizes = [
-        -(-(5 + (half_lat // fifths) * (fifth + 1) - 1) // BLK) for fifth in range(fifths)
-    ]
     place = jnp.stack([lax.axis_index("lat"), lax.axis_index("lev")]).astype(jnp.int32)
     pairs = [(lev, lev ^ 1) for lev in range(levs)]
     same_core = [[2 * chip + core for chip in range(chips)] for core in range(2)]
     rows = slots * fifths * 16
 
-    packed = pl.pallas_call(
-        pack_kernel,
-        out_shape=jax.ShapeDtypeStruct((slots * (2 * fifths * cols + 2 * fields), BLK), BF16),
-        in_specs=[SMEM, ANY, ANY],
-        out_specs=VMEM,
-        scratch_shapes=[
-            pltpu.VMEM(spec_in.shape, BF16),
-            pltpu.SemaphoreType.DMA((1 + slots * 2 * fifths,)),
+    half = half_lat // 2
+    packed = jnp.concatenate(
+        [
+            jnp.where(lax.axis_index("lev") & 1 == 0, legendre[:, :, half:], legendre[:, :, :half]),
+            jnp.pad(
+                spec_in.reshape(slots, 2 * fields, cols),
+                ((0, 0), (0, cols - 2 * fields), (0, BLK - cols)),
+            ),
         ],
-        compiler_params=params(16),
-        name="pack",
-    )(place, spec_in, legendre)
+        axis=2,
+    )
     packed = lax.ppermute(packed, "lev", pairs)
 
-    table, turns, weights, mix, own = pl.pallas_call(
-        lambda *refs: table_kernel(sizes, lats, chips, half_lat, *refs),
+    table, turns, weights, mix, grams, own = pl.pallas_call(
+        lambda *refs: table_kernel(fifths, *refs),
         out_shape=(
-            jax.ShapeDtypeStruct((2 * waves, sum(sizes) * BLK), BF16),
+            jax.ShapeDtypeStruct((2 * waves, sum(widths(1, fifths)) + fifths * BLK), BF16),
             jax.ShapeDtypeStruct((4, waves, BLK), F32),
             jax.ShapeDtypeStruct((8, BLK), F32),
             jax.ShapeDtypeStruct((8 * fields, 8 * fields), BF16),
+            jax.ShapeDtypeStruct((fifths, 2 * waves, BLK), BF16),
             jax.ShapeDtypeStruct((slots, cols, fifths * 2 * BLK), BF16),
         ),
         in_specs=[SMEM, SMEM, SMEM, VMEM, ANY],
-        out_specs=(VMEM,) * 5,
-        scratch_shapes=[pltpu.SemaphoreType.DMA((slots * fifths,))],
-        compiler_params=params(16),
+        out_specs=(VMEM,) * 6,
+        scratch_shapes=[pltpu.SemaphoreType.DMA((slots,))],
+        compiler_params=params(),
         cost_estimate=pl.CostEstimate(flops=20_000_000, bytes_accessed=4_000_000, transcendentals=0),
         name="tables",
     )(place, deal_list, circle_lengths, mixing, legendre)
@@ -375,7 +389,7 @@
         ),
         in_specs=[SMEM, SMEM, VMEM, VMEM, VMEM],
         out_specs=(VMEM, VMEM),
-        compiler_params=params(16),
+        compiler_params=params(),
         name="inverse",
     )(place, deal_list, spec_in, own, packed)
     parts = lax.all_to_all(
@@ -387,19 +401,24 @@
         in_specs=[VMEM],
         out_specs=VMEM,
         scratch_shapes=[pltpu.VMEM((lats * 16, BLK), F32)],
-        compiler_params=params(16),
+        compiler_params=params(),
         name="sums",
     )(parts)
     fourier = lax.all_to_all(fourier, "lat", 0, 0, tiled=True)
     analysed = pl.pallas_call(
-        lambda *refs: grid_kernel(sizes, (2.0 * waves) ** (-0.5), *refs),
+        lambda *refs: grid_kernel((2.0 * waves) ** (-0.5), *refs),
         out_shape=jax.ShapeDtypeStruct((lats, 16, BLK), BF16),
-        in_specs=[VMEM] * 5,
+        in_specs=[SMEM, SMEM] + [VMEM] * 6,
         out_specs=VMEM,
-        scratch_shapes=[pltpu.VMEM((lats * 16, BLK), F32), pltpu.VMEM((lats * 16, BLK), F32)],
-        compiler_params=params(24),
+        scratch_shapes=[
+            pltpu.VMEM((lats * 16, BLK), F32),
+            pltpu.VMEM((lats * 16, BLK), F32),
+            pltpu.VMEM((fifths, 2 * waves, 8 * fields), F32),
+            pltpu.VMEM((fifths, 8 * fields, BLK), BF16),
+        ],
+        compiler_params=params(24576),
         name="grid_rows",
-    )(fourier, table, turns, weights, mix)
+    )(place, circle_lengths, fourier, table, turns, weights, mix, grams)
     analysed = lax.all_to_all(analysed, "lat", 0, 0, tiled=True)
     copies = pl.pallas_call(
         copies_kernel,
@@ -407,7 +426,7 @@
         in_specs=[VMEM],
         out_specs=VMEM,
         scratch_shapes=[pltpu.VMEM((lats * 16, BLK), F32)],
-        compiler_params=params(16),
+        compiler_params=params(),
         name="copies",
     )(analysed)
     gathered = lax.all_to_all(copies, "lev", 0, 0, tiled=True, axis_index_groups=same_core)
@@ -418,7 +437,7 @@
             out_shape=jax.ShapeDtypeStruct((slots, 2, fields, cols), F32),
             in_specs=[SMEM, VMEM, VMEM],
             out_specs=VMEM,
-            compiler_params=params(16),
+            compiler_params=params(),
             cost_estimate=pl.CostEstimate(
                 flops=100_000_000, bytes_accessed=2_000_000, transcendentals=0
             ),

time: 98.5 us -> 96.1 us (0.976)
  other arithmetic: 0.72 us -> 2.75 us
  local copies, waits for them, and re-layouts: 1.92 us -> 0.02 us
  Pallas kernels: 12.3 us -> 10.6 us
  starting transfers between devices: 15.8 us -> 14.3 us
    unnamed x12 -> x10, local copies, waits for them, and re-layouts: 1.92 us -> 0.02 us
    pallas_call x3 -> x2, Pallas kernels: 9.08 us -> 7.38 us  [the longest x1 4.6 us: local(): pl.pallas_call(lambda *refs: grid_kernel((2.0 * waves) ** (-0.5), *refs),...]
    ppermute x1, starting transfers between devices: 7 us -> 5.56 us  [local(): share = lax.ppermute(direct(False, other), 'lev', pairs)]
    select_n x0 -> x1, other arithmetic: none -> 1.24 us  [local(): jnp.where(lax.axis_index('lev') & 1 == 0, legendre[:, :, half:], legendre...]
  transfers between devices with their start and end apart: 2 -> 2, of which waited for: 0 -> 0; matrix products, arithmetic and copies ran while one was open for 0% -> 0% of each run, Pallas kernels for 3% -> 4%
where the time goes in v3:
time: 96.1 us; the launch traced here: 95.7 us
  blocking collectives  67.9 us (71%)
  starting transfers between devices  14.3 us (15%)
  Pallas kernels  10.6 us (11%)
  other arithmetic  2.75 us (3%)
    all_to_all x1, blocking collectives, local(): fourier = lax.all_to_all(fourier, 'lat', 0, 0, tiled=True)  24.7 us
    all_to_all x1, blocking collectives, local(): lax.all_to_all(partial_sums, 'lev', 0, 0, tiled=True, axis_index_groups=s...  15.7 us
    all_to_all x1, blocking collectives, local(): analysed = lax.all_to_all(analysed, 'lat', 0, 0, tiled=True)  14.5 us
    all_to_all x1, blocking collectives, local(): lax.all_to_all(copies, 'lev', 0, 0, tiled=True, axis_index_groups=same_core)  13.1 us
    ppermute x1, starting transfers between devices, local(): packed = lax.ppermute(packed, 'lev', pairs)  8.77 us
    ppermute x1, starting transfers between devices, local(): share = lax.ppermute(direct(False, other), 'lev', pairs)  5.56 us
    pallas_call x1, Pallas kernels, local(): pl.pallas_call(lambda *refs: grid_kernel((2.0 * waves) ** (-0.5), *refs),...  4.6 us
    pallas_call x1, Pallas kernels, local(): pl.pallas_call(lambda *refs: table_kernel(fifths, *refs), out_shape=(jax....  2.78 us
  transfers between devices with their start and end apart: 2, of which 0 were waited for; matrix products, arithmetic and copies ran while one was open for 0% of the time, Pallas kernels for 4%

profile of v3, /device:TPU:1, one launch (start us, length us, event | category | flops | bytes accessed | tf_op | source)
XLA Modules:
  0.0 95.7 jit_solution(8610563591582651486)
XLA Ops:
  0.0 0.0 copy-start
  0.0 0.0 copy-start.2
  0.0 0.0 copy-start.4
  0.0 0.0 copy-start.3
  0.0 0.0 copy-start.1
  0.0 1.2 %slice_select_fusion = bf16[2,80,1280]{2,1,0:T(8,128)(2,1)S(1)} fusion(bf16[2,80,2560]{2,1,0:T(8,128)(2,1)} %refs_4_.1, pred[]{:T(512)S(6)} %eq.3), kind=kLoop, calls=%fused_computation.3 | loop fusion | flops 204800 | bytes 1228801 | tf_op jit(solution)/shard_map/jit(_where)/select_n | solution.py:356
  1.3 0.8 fusion.1
  2.1 8.8 %collective-permute-start = (bf16[2,80,1408]{2,1,0:T(8,128)(2,1)S(1)}, bf16[2,80,1408]{2,1,0:T(8,128)(2,1)S(1)}, u32[]{:S(2)}, u32[]{:S(2)}) collective-permute-start(bf16[2,80,1408]{2,1,0:T(8,128)(2,1)S(1)} %fusion.1), channel_id=1, source_target_pairs={{0,1},{1,0},{2,3},{3,2},{4,5},{5,4},{6,7},{7,6},{8,9},{9,8},{10,11... | collective-permute-start | bytes 1351688 | tf_op jit(solution)/shard_map/ppermute | solution.py:364
  10.9 0.1 pad_add_fusion.refs_0_.place_ref
  10.9 0.0 copy-done
  10.9 0.0 copy-done.2
  10.9 0.0 copy-done.4
  10.9 0.0 copy-done.3
  11.0 2.8 %tables.1 = (bf16[64,10880]{1,0:T(8,128)(2,1)S(1)}, f32[4,32,128]{2,1,0:T(8,128)S(1)}, f32[8,128]{1,0:T(8,128)S(1)}, bf16[256,256]{1,0:T(8,128)(2,1)S(1)}, bf16[...) custom-call(s32[2]{0:T(128)S(1)} %pad_add_fusion.refs_0_.place_ref, s32[32]{0:T(128)S(1)} %copy-done.4, ...), custom_call_target="tpu_custom_call" | custom-call | flops 20000000 | bytes 4000000 | tf_op jit(solution)/shard_map/tables/pallas_call | solution.py:366
  13.7 0.0 collective-permute-done.packed_ref
  13.7 0.0 copy-done.1
  13.8 1.2 %inverse.1 = (bf16[16,160,128]{2,1,0:T(8,128)(2,1)S(1)}, bf16[2,80,1280]{2,1,0:T(8,128)(2,1)S(1)}) custom-call(s32[2]{0:T(128)S(1)} %pad_add_fusion.refs_0_.place_ref, s32[32]{0:T(128)S(1)} %copy-done.4, bf16[2,2,32,80]{3,2,1,0:T(8,128)(2,1)S(1)} %copy-done.1, bf16[2,80,1280]{2,1,0:T(8,128)(2,1)S(1)} %get-tuple-element.13.own_ref.refs_2_, ...), custom_call_target="tpu_custom_call" | custom-call | tf_op jit(solution)/shard_map/inverse/pallas_call | solution.py:384
  15.0 15.7 %all_to_all.20.in_ref = bf16[16,160,128]{2,1,0:T(8,128)(2,1)S(1)} all-to-all(bf16[16,160,128]{2,1,0:T(8,128)(2,1)S(1)} %get-tuple-element.14), channel_id=1, replica_groups={{0,2,4,6,8,10,12,14,16,18,20,22,24,26,28,30},{1,3,5,7,9,11,13,15,17,19,..., dimensions={0} | all-to-all | bytes 1310720 | tf_op jit(solution)/shard_map/all_to_all | solution.py:395
  30.7 0.1 sums.1
  30.8 24.7 %all_to_all.21.refs_2_ = bf16[16,16,128]{2,1,0:T(8,128)(2,1)S(1)} all-to-all(bf16[16,16,128]{2,1,0:T(8,128)(2,1)S(1)} %sums.1), channel_id=1, replica_groups=mesh['lat'=16,'lev'=32] {'lat'}, dimensions={0} | all-to-all | bytes 131072 | tf_op jit(solution)/shard_map/all_to_all | solution.py:407
  55.4 4.6 %grid_rows.1 = bf16[16,16,128]{2,1,0:T(8,128)(2,1)S(1)} custom-call(s32[2]{0:T(128)S(1)} %pad_add_fusion.refs_0_.place_ref, s32[2560]{0:T(1024)S(1)} %copy-done.2, bf16[16,16,128]{2,1,0:T(8,128)(2,1)S(1)} %all_to_all.21.refs_2_, bf16[64,10880]{1,0:T(8,128)(2,1)S(1)} %get-tuple-element.15.refs_3_, f32[4,32,128]{2,1,0:T(8,128)S(1)} %get-tuple-element.16.refs_4_, ...), custom_call_target="tpu_custom_call" | custom-call | tf_op jit(solution)/shard_map/grid_rows/pallas_call | solution.py:408
  60.0 14.5 %all_to_all.22.in_ref = bf16[16,16,128]{2,1,0:T(8,128)(2,1)S(1)} all-to-all(bf16[16,16,128]{2,1,0:T(8,128)(2,1)S(1)} %grid_rows.1), channel_id=1, replica_groups=mesh['lat'=16,'lev'=32] {'lat'}, dimensions={0} | all-to-all | bytes 131072 | tf_op jit(solution)/shard_map/all_to_all | solution.py:422
  74.5 0.1 copies.1
  74.6 13.1 %all_to_all.23.refs_1_ = bf16[16,160,128]{2,1,0:T(8,128)(2,1)S(1)} all-to-all(bf16[16,160,128]{2,1,0:T(8,128)(2,1)S(1)} %copies.1), channel_id=1, replica_groups={{0,2,4,6,8,10,12,14,16,18,20,22,24,26,28,30},{1,3,5,7,9,11,13,15,17,19,..., dimensions={0} | all-to-all | bytes 1310720 | tf_op jit(solution)/shard_map/all_to_all | solution.py:432
  87.6 0.9 direct_other.1
  88.6 5.6 %collective-permute-start.1 = (f32[2,2,32,80]{3,2,1,0:T(8,128)S(1)}, f32[2,2,32,80]{3,2,1,0:T(8,128)S(1)}, u32[]{:S(2)}, u32[]{:S(2)}) collective-permute-start(f32[2,2,32,80]{3,2,1,0:T(8,128)S(1)} %direct_other.1), channel_id=1, source_target_pairs={{0,1},{1,0},{2,3},{3,2},{4,5},{5,4},{6,7},{7,6},{8,9},{9,8},{10,11... | collective-permute-start | bytes 122888 | tf_op jit(solution)/shard_map/ppermute | solution.py:447
  94.1 0.9 direct_own.1
  95.1 0.0 collective-permute-done.1
  95.1 0.6 add.5
Async XLA Ops:
  0.0 10.9 %copy-start = (bf16[2,80,2560]{2,1,0:T(8,128)(2,1)S(1)}, bf16[2,80,2560]{2,1,0:T(8,128)(2,1)}, u32[]{:S(2)}) copy-start(bf16[2,80,2560]{2,1,0:T(8,128)(2,1)} %refs_4_.1) | copy-start | bytes 2457604
  0.0 10.9 %copy-start.2 = (s32[2560]{0:T(1024)S(1)}, s32[2560]{0:T(1024)}, u32[]{:S(2)}) copy-start(s32[2560]{0:T(1024)} %refs_1_.3) | copy-start | bytes 30724
  0.0 10.9 %copy-start.4 = (s32[32]{0:T(128)S(1)}, s32[32]{0:T(128)}, u32[]{:S(2)}) copy-start(s32[32]{0:T(128)} %deal_ref.1) | copy-start | bytes 388
  0.0 10.9 %copy-start.3 = (bf16[32,32]{1,0:T(8,128)(2,1)S(1)}, bf16[32,32]{1,0:T(8,128)(2,1)}, u32[]{:S(2)}) copy-start(bf16[32,32]{1,0:T(8,128)(2,1)} %refs_3_.1) | copy-start | bytes 6148
  0.0 13.7 %copy-start.1 = (bf16[2,2,32,80]{3,2,1,0:T(8,128)(2,1)S(1)}, bf16[2,2,32,80]{3,2,1,0:T(8,128)(2,1)}, u32[]{:S(2)}) copy-start(bf16[2,2,32,80]{3,2,1,0:T(8,128)(2,1)} %spec_ref.1) | copy-start | bytes 61444
  2.1 11.7 %collective-permute-start = (bf16[2,80,1408]{2,1,0:T(8,128)(2,1)S(1)}, bf16[2,80,1408]{2,1,0:T(8,128)(2,1)S(1)}, u32[]{:S(2)}, u32[]{:S(2)}) collective-permute-start(bf16[2,80,1408]{2,1,0:T(8,128)(2,1)S(1)} %fusion.1), channel_id=1, source_target_pairs={{0,1},{1,0},{2,3},{3,2},{4,5},{5,4},{6,7},{7,6},{8,9},{9,8},{10,11... | collective-permute-start | bytes 1351688 | tf_op jit(solution)/shard_map/ppermute | solution.py:364
  88.6 6.5 %collective-permute-start.1 = (f32[2,2,32,80]{3,2,1,0:T(8,128)S(1)}, f32[2,2,32,80]{3,2,1,0:T(8,128)S(1)}, u32[]{:S(2)}, u32[]{:S(2)}) collective-permute-start(f32[2,2,32,80]{3,2,1,0:T(8,128)S(1)} %direct_other.1), channel_id=1, source_target_pairs={{0,1},{1,0},{2,3},{3,2},{4,5},{5,4},{6,7},{7,6},{8,9},{9,8},{10,11... | collective-permute-start | bytes 122888 | tf_op jit(solution)/shard_map/ppermute | solution.py:447

commit v4 on v3

--- a/solution.py
+++ b/solution.py
@@ -13,13 +13,18 @@
 F32 = jnp.float32
 BF16 = jnp.bfloat16
 VMEM = pl.BlockSpec(memory_space=pltpu.VMEM)
-ANY = pl.BlockSpec(memory_space=pl.ANY)
 SMEM = pl.BlockSpec(memory_space=pltpu.SMEM)
 NT = (((1,), (1,)), ((), ()))
 
 
 def params(kib=16384):
     return pltpu.CompilerParams(vmem_limit_bytes=kib * 1024)
+
+
+def wave_of(deal_ref, slot):
+    deal = deal_ref[...]
+    here = lax.broadcasted_iota(jnp.int32, deal.shape, 1) == slot
+    return jnp.sum(jnp.where(here, deal, 0).astype(F32), axis=1, keepdims=True).astype(jnp.int32)
 
 
 def live_degrees(wave, first_col, shape):
@@ -33,8 +38,8 @@
     return jnp.where(flags, value, jnp.zeros_like(value))
 
 
-def inverse_kernel(place_ref, deal_ref, spec_ref, own_ref, packed_ref, out_ref, other_ref):
-    lat, lev = place_ref[0], place_ref[1]
+def inverse_kernel(deal_ref, spec_ref, own_ref, packed_ref, out_ref, other_ref):
+    lat, lev = lax.axis_index("lat"), lax.axis_index("lev")
     core = lax.rem(lev, 2)
     slots, _, fields, cols = spec_ref.shape
     chips = out_ref.shape[0]
@@ -53,7 +58,7 @@
 
     half_rows = fifths * 2 * BLK
     for slot in range(slots):
-        wave = deal_ref[slots * lat + slot]
+        wave = wave_of(deal_ref, slots * lat + slot)
         live = live_degrees(wave, theirs, (cols, BLK))
         left = stacked([spec_ref[slot, part] for part in range(2)], mine)
         other_left = stacked(
@@ -137,21 +142,28 @@
     return [2 * BLK * (core * fifths + fifth + 1) for fifth in range(fifths)]
 
 
-def table_kernel(fifths, place_ref, deal_ref, lengths_ref, mixing_ref, leg_ref,
-                 table_ref, turn_ref, weight_ref, mix_ref, gram_ref, own_ref, sems):
-    lat, lev = place_ref[0], place_ref[1]
+def own_kernel(deal_ref, leg_ref, own_ref):
+    lat, lev = lax.axis_index("lat"), lax.axis_index("lev")
     core = lax.rem(lev, 2)
-    slots, cols, half_lat = leg_ref.shape
+    slots, cols, half_rows = own_ref.shape
+    blocks = half_rows // BLK
+    for slot in range(slots):
+        wave = wave_of(deal_ref, slots * lat + slot)
+        live = live_degrees(wave, lev * cols, (cols, BLK))
+        for block in range(blocks):
+            row_block = blocks * core + block
+            value = leg_ref[slot, :, pl.ds(pl.multiple_of(row_block * BLK, BLK), BLK)]
+            own_ref[slot, :, block * BLK : (block + 1) * BLK] = mask_rows(
+                value, wave, live, row_block, 2 * blocks
+            )
+
+
+def table_kernel(fifths, deal_ref, lengths_ref, mixing_ref,
+                 table_ref, turn_ref, weight_ref, mix_ref, gram_ref):
+    lat, lev = lax.axis_index("lat"), lax.axis_index("lev")
+    core = lax.rem(lev, 2)
+    half_lat = lengths_ref.shape[0]
     half_rows = half_lat // 2
-    copies = []
-    for slot in range(slots):
-        begin = pl.multiple_of(core * half_rows, BLK)
-        copies.append(
-            pltpu.make_async_copy(
-                leg_ref.at[slot, :, pl.ds(begin, half_rows)], own_ref.at[slot], sems.at[slot]
-            )
-        )
-        copies[-1].start()
     waves = deal_ref.shape[0]
     fields = mixing_ref.shape[0]
     shape = (waves, BLK)
@@ -187,10 +199,12 @@
         main = widths(which, fifths)
         extra = sum(main)
         start = 0
+        beyond = 0
         for fifth, width in enumerate(main):
             row = first_row + fifth * group
             length = lengths_ref[row]
             points = length // 4
+            beyond = jnp.maximum(beyond, points - width)
             length_f = jnp.full(shape, length, jnp.int32).astype(F32)
             low_cos, low_sin = circle(wave_f * lane_f, length_f)
             high_cos, high_sin = circle(wave_f * lane_f * float(BLK), length_f)
@@ -209,6 +223,7 @@
             _, sine = circle(row_f, jnp.full((1, BLK), 4.0 * half_lat, F32))
             weight_ref[fifth : fifth + 1, :] = sine / jnp.sqrt(length_f[0:1, :])
             start += width
+        weight_ref[fifths : fifths + 1, :] = jnp.full((1, BLK), beyond, jnp.int32).astype(F32)
         start = 0
         for fifth, width in enumerate(main):
             table = table_ref[:, start : start + width]
@@ -220,17 +235,6 @@
 
     pl.when(core == 0)(lambda: build(0))
     pl.when(core == 1)(lambda: build(1))
-    for copy in copies:
-        copy.wait()
-    for slot in range(slots):
-        number = deal_ref[slots * lat + slot]
-        live = live_degrees(number, lev * cols, (cols, BLK))
-        for block in range(2 * fifths):
-            here = slice(block * BLK, (block + 1) * BLK)
-            row_block = 2 * fifths * core + block
-            own_ref[slot, :, here] = mask_rows(
-                own_ref[slot, :, here], number, live, row_block, 4 * fifths
-            )
 
 
 def two_terms(value):
@@ -239,18 +243,17 @@
     return jnp.concatenate([high, low], axis=1)
 
 
-def grid_kernel(scale, place_ref, lengths_ref, in_ref, table_ref, turn_ref, weight_ref, mix_ref, gram_ref,
+def grid_kernel(scale, in_ref, table_ref, turn_ref, weight_ref, mix_ref, gram_ref,
                 out_ref, spread, gathered, totals, mixed_coeffs):
     fifths = gram_ref.shape[0]
     waves = turn_ref.shape[1]
-    core = lax.rem(place_ref[1], 2)
+    core = lax.rem(lax.axis_index("lev"), 2)
+    beyond = jnp.max(weight_ref[fifths : fifths + 1, :])
     lane = lax.broadcasted_iota(jnp.int32, (waves, BLK), 1)
     front = lane < BLK // 2
     spread[...] = in_ref[...].astype(F32).reshape(spread.shape)
     gathered[...] = jnp.zeros_like(gathered)
     mix = mix_ref[...]
-    group = 2 * BLK
-    first_row = core * fifths * group + (place_ref[1] // 2) * (group // CHIPS) + place_ref[0]
 
     def analysed(table, fifth):
         twice = jnp.concatenate([table, table], axis=0)
@@ -288,12 +291,10 @@
                 total = total + analysed(table_ref[:, begin:end], fifth)
             totals[fifth] = total
             start += width
-        for fifth, width in enumerate(main):
-            begin = start + fifth * BLK
-            points = lengths_ref[first_row + fifth * group] // 4
-
-            @pl.when(points > width)
-            def _():
+        @pl.when(beyond > 0.0)
+        def _():
+            for fifth in range(fifths):
+                begin = start + fifth * BLK
                 totals[fifth] += analysed(table_ref[:, begin : begin + BLK], fifth)
 
     pl.when(core == 0)(lambda: rows(0))
@@ -316,8 +317,8 @@
     out_ref[...] = gathered[...].astype(BF16).reshape(out_ref.shape)
 
 
-def direct_kernel(mine, place_ref, rows_ref, live_ref, out_ref):
-    lev = place_ref[1]
+def direct_kernel(mine, rows_ref, live_ref, out_ref):
+    lev = lax.axis_index("lev")
     owner = lev if mine else lev + 1 - 2 * lax.rem(lev, 2)
     slots, cols, _ = live_ref.shape
     fields = out_ref.shape[2]
@@ -345,11 +346,11 @@
     fields = spec_in.shape[2]
     waves = deal_list.shape[0]
     fifths = half_lat // (lats * levs)
-    place = jnp.stack([lax.axis_index("lat"), lax.axis_index("lev")]).astype(jnp.int32)
     pairs = [(lev, lev ^ 1) for lev in range(levs)]
     same_core = [[2 * chip + core for chip in range(chips)] for core in range(2)]
     rows = slots * fifths * 16
 
+    deal_row = deal_list.reshape(1, waves)
     half = half_lat // 2
     packed = jnp.concatenate(
         [
@@ -363,7 +364,7 @@
     )
     packed = lax.ppermute(packed, "lev", pairs)
 
-    table, turns, weights, mix, grams, own = pl.pallas_call(
+    table, turns, weights, mix, grams = pl.pallas_call(
         lambda *refs: table_kernel(fifths, *refs),
         out_shape=(
             jax.ShapeDtypeStruct((2 * waves, sum(widths(1, fifths)) + fifths * BLK), BF16),
@@ -371,15 +372,22 @@
             jax.ShapeDtypeStruct((8, BLK), F32),
             jax.ShapeDtypeStruct((8 * fields, 8 * fields), BF16),
             jax.ShapeDtypeStruct((fifths, 2 * waves, BLK), BF16),
-            jax.ShapeDtypeStruct((slots, cols, fifths * 2 * BLK), BF16),
         ),
-        in_specs=[SMEM, SMEM, SMEM, VMEM, ANY],
-        out_specs=(VMEM,) * 6,
-        scratch_shapes=[pltpu.SemaphoreType.DMA((slots,))],
+        in_specs=[SMEM, SMEM, VMEM],
+        out_specs=(VMEM,) * 5,
         compiler_params=params(),
         cost_estimate=pl.CostEstimate(flops=20_000_000, bytes_accessed=4_000_000, transcendentals=0),
         name="tables",
-    )(place, deal_list, circle_lengths, mixing, legendre)
+    )(deal_list, circle_lengths, mixing)
+    own = pl.pallas_call(
+        own_kernel,
+        out_shape=jax.ShapeDtypeStruct((slots, cols, fifths * 2 * BLK), BF16),
+        in_specs=[VMEM, VMEM],
+        out_specs=VMEM,
+        compiler_params=params(),
+        cost_estimate=pl.CostEstimate(flops=1_000_000, bytes_accessed=1_300_000, transcendentals=0),
+        name="own",
+    )(deal_row, legendre)
 
     partial_sums, other = pl.pallas_call(
         inverse_kernel,
@@ -387,11 +395,11 @@
             jax.ShapeDtypeStruct((chips, rows, BLK), BF16),
             jax.ShapeDtypeStruct((slots, cols, fifths * 2 * BLK), BF16),
         ),
-        in_specs=[SMEM, SMEM, VMEM, VMEM, VMEM],
+        in_specs=[VMEM] * 4,
         out_specs=(VMEM, VMEM),
         compiler_params=params(),
         name="inverse",
-    )(place, deal_list, spec_in, own, packed)
+    )(deal_row, spec_in, own, packed)
     parts = lax.all_to_all(
         partial_sums, "lev", 0, 0, tiled=True, axis_index_groups=same_core
     )
@@ -408,7 +416,7 @@
     analysed = pl.pallas_call(
         lambda *refs: grid_kernel((2.0 * waves) ** (-0.5), *refs),
         out_shape=jax.ShapeDtypeStruct((lats, 16, BLK), BF16),
-        in_specs=[SMEM, SMEM] + [VMEM] * 6,
+        in_specs=[VMEM] * 6,
         out_specs=VMEM,
         scratch_shapes=[
             pltpu.VMEM((lats * 16, BLK), F32),
@@ -418,7 +426,7 @@
         ],
         compiler_params=params(24576),
         name="grid_rows",
-    )(place, circle_lengths, fourier, table, turns, weights, mix, grams)
+    )(fourier, table, turns, weights, mix, grams)
     analysed = lax.all_to_all(analysed, "lat", 0, 0, tiled=True)
     copies = pl.pallas_call(
         copies_kernel,
@@ -435,14 +443,14 @@
         return pl.pallas_call(
             lambda *refs: direct_kernel(mine, *refs),
             out_shape=jax.ShapeDtypeStruct((slots, 2, fields, cols), F32),
-            in_specs=[SMEM, VMEM, VMEM],
+            in_specs=[VMEM, VMEM],
             out_specs=VMEM,
             compiler_params=params(),
             cost_estimate=pl.CostEstimate(
                 flops=100_000_000, bytes_accessed=2_000_000, transcendentals=0
             ),
             name="direct_own" if mine else "direct_other",
-        )(place, gathered, live)
+        )(gathered, live)
 
     share = lax.ppermute(direct(False, other), "lev", pairs)
     return direct(True, own) + share

time: 96.1 us -> 93 us (0.968)
  blocking collectives: 67.9 us -> 42.6 us
  starting transfers between devices: 14.3 us -> 27.7 us
  waiting for transfers between devices: 0.01 us -> 10.6 us
  Pallas kernels: 10.6 us -> 8.9 us
    all_to_all x1 -> x0, blocking collectives: 24.7 us -> none  [local(): fourier = lax.all_to_all(fourier, 'lat', 0, 0, tiled=True)]
    all_to_all x0 -> x1, starting transfers between devices: none -> 13.2 us  [local(): fourier = lax.all_to_all(fourier, 'lat', 0, 0, tiled=True)]
    all_to_all x0 -> x1, waiting for transfers between devices: none -> 9.11 us  [local(): fourier = lax.all_to_all(fourier, 'lat', 0, 0, tiled=True)]
    pallas_call x2, Pallas kernels: 1.89 us -> 0.81 us  [direct(): pl.pallas_call(lambda *refs: direct_kernel(mine, *refs), out_shape=jax.Sh...]
    ppermute x1, waiting for transfers between devices: 0.01 us -> 1.05 us  [local(): packed = lax.ppermute(packed, 'lev', pairs)]
  transfers between devices with their start and end apart: 2 -> 3, of which waited for: 0 -> 3; matrix products, arithmetic and copies ran while one was open for 0% -> 0% of each run, Pallas kernels for 4% -> 3%
where the time goes in v4:
time: 93 us; the launch traced here: 92.6 us
  blocking collectives  42.6 us (46%)
  starting transfers between devices  27.7 us (30%)
  waiting for transfers between devices  10.6 us (11%)
  Pallas kernels  8.9 us (10%)
  other arithmetic  2.68 us (3%)
    all_to_all x1, blocking collectives, local(): lax.all_to_all(partial_sums, 'lev', 0, 0, tiled=True, axis_index_groups=s...  14.9 us
    all_to_all x1, blocking collectives, local(): analysed = lax.all_to_all(analysed, 'lat', 0, 0, tiled=True)  14.4 us
    all_to_all x1, blocking collectives, local(): lax.all_to_all(copies, 'lev', 0, 0, tiled=True, axis_index_groups=same_core)  13.3 us
    all_to_all x1, starting transfers between devices, local(): fourier = lax.all_to_all(fourier, 'lat', 0, 0, tiled=True)  13.2 us
    all_to_all x1, waiting for transfers between devices, local(): fourier = lax.all_to_all(fourier, 'lat', 0, 0, tiled=True)  9.11 us
    ppermute x1, starting transfers between devices, local(): packed = lax.ppermute(packed, 'lev', pairs)  8.78 us
    ppermute x1, starting transfers between devices, local(): share = lax.ppermute(direct(False, other), 'lev', pairs)  5.68 us
    pallas_call x1, Pallas kernels, local(): pl.pallas_call(lambda *refs: grid_kernel((2.0 * waves) ** (-0.5), *refs),...  3.85 us
  transfers between devices with their start and end apart: 3, of which 3 were waited for; matrix products, arithmetic and copies ran while one was open for 0% of the time, Pallas kernels for 3%

profile of v4, /device:TPU:1, one launch (start us, length us, event | category | flops | bytes accessed | tf_op | source)
XLA Modules:
  0.0 92.6 jit_solution(12270238162155206916)
XLA Ops:
  0.0 0.0 copy-start
  0.0 0.0 copy-start.2
  0.0 0.0 copy-start.1
  0.0 1.2 %slice_select_fusion = bf16[2,80,1280]{2,1,0:T(8,128)(2,1)S(1)} fusion(bf16[2,80,2560]{2,1,0:T(8,128)(2,1)} %leg_ref.1, pred[]{:T(512)S(6)} %eq.3), kind=kLoop, calls=%fused_computation.3 | loop fusion | flops 204800 | bytes 1228801 | tf_op jit(solution)/shard_map/jit(_where)/select_n | solution.py:357
  1.3 0.8 fusion.1
  2.1 8.8 %collective-permute-start = (bf16[2,80,1408]{2,1,0:T(8,128)(2,1)S(1)}, bf16[2,80,1408]{2,1,0:T(8,128)(2,1)S(1)}, u32[]{:S(2)}, u32[]{:S(2)}) collective-permute-start(bf16[2,80,1408]{2,1,0:T(8,128)(2,1)S(1)} %fusion.1), channel_id=1, source_target_pairs={{0,1},{1,0},{2,3},{3,2},{4,5},{5,4},{6,7},{7,6},{8,9},{9,8},{10,11... | collective-permute-start | bytes 1351688 | tf_op jit(solution)/shard_map/ppermute | solution.py:365
  10.8 0.0 copy-done
  10.9 0.0 copy-done.2
  10.9 0.3 own.1.own_ref.refs_1_
  11.2 0.0 copy-start.3
  11.2 0.0 copy-start.4
  11.2 1.0 %collective-permute-done.packed_ref = bf16[2,80,1408]{2,1,0:T(8,128)(2,1)S(1)} collective-permute-done((bf16[2,80,1408]{2,1,0:T(8,128)(2,1)S(1)}, bf16[2,80,1408]{2,1,0:T(8,128)(2,1)S(1)}, u32[]{:S(2)}, u32[]{:S(2)}) %collective-permute-start) | collective-permute-done | bytes 450592 | tf_op jit(solution)/shard_map/ppermute | solution.py:365
  12.3 0.0 copy-done.1
  12.3 0.7 inverse.1
  13.0 14.9 %all_to_all.20.in_ref = bf16[16,160,128]{2,1,0:T(8,128)(2,1)S(1)} all-to-all(bf16[16,160,128]{2,1,0:T(8,128)(2,1)S(1)} %get-tuple-element.12), channel_id=1, replica_groups={{0,2,4,6,8,10,12,14,16,18,20,22,24,26,28,30},{1,3,5,7,9,11,13,15,17,19,..., dimensions={0} | all-to-all | bytes 1310720 | tf_op jit(solution)/shard_map/all_to_all | solution.py:403
  27.8 0.7 sums.1
  28.6 13.2 %all-to-all-start.1 = ((bf16[16,16,128]{2,1,0:T(8,128)(2,1)}), bf16[16,16,128]{2,1,0:T(8,128)(2,1)S(1)}, u32[]{:S(2)}, u32[]{:S(2)}) async-start(bf16[16,16,128]{2,1,0:T(8,128)(2,1)} %sums.1), calls=%async_computation.1 | async-start | bytes 131072 | tf_op jit(solution)/shard_map/all_to_all | solution.py:415
  41.8 0.0 copy-done.3
  41.8 0.0 copy-done.4
  41.8 2.4 %tables.1 = (bf16[64,10880]{1,0:T(8,128)(2,1)S(1)}, f32[4,32,128]{2,1,0:T(8,128)S(1)}, f32[8,128]{1,0:T(8,128)S(1)}, bf16[256,256]{1,0:T(8,128)(2,1)S(1)}, bf16[5,64,128]{2,1,0:T(8,128)(2,1)S(1)}) custom-call(s32[32]{0:T(128)S(1)} %copy-done.2, s32[2560]{0:T(1024)S(1)} %copy-done.3, bf16[32,32]{1,0:T(8,128)(2,1)S(1)} %copy-done.4), custom_call_target="tpu_custom_call" | custom-call | flops 20000000 | bytes 4000000 | tf_op jit(solution)/shard_map/tables/pallas_call | solution.py:367
  44.2 9.1 %all-to-all-done.1.refs_0_ = bf16[16,16,128]{2,1,0:T(8,128)(2,1)S(1)} async-done(((bf16[16,16,128]{2,1,0:T(8,128)(2,1)}), bf16[16,16,128]{2,1,0:T(8,128)(2,1)S(1)}, u32[]{:S(2)}, u32[]{:S(2)}) %all-to-all-start.1) | async-done | bytes 65568 | tf_op jit(solution)/shard_map/all_to_all | solution.py:415
  53.3 3.9 %grid_rows.1 = bf16[16,16,128]{2,1,0:T(8,128)(2,1)S(1)} custom-call(bf16[16,16,128]{2,1,0:T(8,128)(2,1)S(1)} %all-to-all-done.1.refs_0_, bf16[64,10880]{1,0:T(8,128)(2,1)S(1)} %get-tuple-element.13.refs_1_, f32[4,32,128]{2,1,0:T(8,128)S(1)} %get-tuple-element.14.refs_2_, f32[8,128]{1,0:T(8,128)S(1)} %get-tuple-element.15.refs_3_, ...), custom_call_target="tpu_custom_call" | custom-call | tf_op jit(solution)/shard_map/grid_rows/pallas_call | solution.py:416
  57.2 14.4 %all_to_all.21.in_ref = bf16[16,16,128]{2,1,0:T(8,128)(2,1)S(1)} all-to-all(bf16[16,16,128]{2,1,0:T(8,128)(2,1)S(1)} %grid_rows.1), channel_id=1, replica_groups=mesh['lat'=16,'lev'=32] {'lat'}, dimensions={0} | all-to-all | bytes 131072 | tf_op jit(solution)/shard_map/all_to_all | solution.py:430
  71.6 0.1 copies.1
  71.7 13.3 %all_to_all.22.refs_0_ = bf16[16,160,128]{2,1,0:T(8,128)(2,1)S(1)} all-to-all(bf16[16,160,128]{2,1,0:T(8,128)(2,1)S(1)} %copies.1), channel_id=1, replica_groups={{0,2,4,6,8,10,12,14,16,18,20,22,24,26,28,30},{1,3,5,7,9,11,13,15,17,19,..., dimensions={0} | all-to-all | bytes 1310720 | tf_op jit(solution)/shard_map/all_to_all | solution.py:440
  85.0 0.4 direct_other.1
  85.4 5.7 %collective-permute-start.1 = (f32[2,2,32,80]{3,2,1,0:T(8,128)S(1)}, f32[2,2,32,80]{3,2,1,0:T(8,128)S(1)}, u32[]{:S(2)}, u32[]{:S(2)}) collective-permute-start(f32[2,2,32,80]{3,2,1,0:T(8,128)S(1)} %direct_other.1), channel_id=1, source_target_pairs={{0,1},{1,0},{2,3},{3,2},{4,5},{5,4},{6,7},{7,6},{8,9},{9,8},{10,11... | collective-permute-start | bytes 122888 | tf_op jit(solution)/shard_map/ppermute | solution.py:455
  91.0 0.4 direct_own.1
  91.4 0.5 collective-permute-done.1
  91.9 0.6 add.5
Async XLA Ops:
  0.0 10.9 %copy-start = (bf16[2,80,2560]{2,1,0:T(8,128)(2,1)S(1)}, bf16[2,80,2560]{2,1,0:T(8,128)(2,1)}, u32[]{:S(2)}) copy-start(bf16[2,80,2560]{2,1,0:T(8,128)(2,1)} %leg_ref.1) | copy-start | bytes 2457604
  0.0 10.9 %copy-start.2 = (s32[32]{0:T(128)S(1)}, s32[32]{0:T(128)}, u32[]{:S(2)}) copy-start(s32[32]{0:T(128)} %refs_0_.1) | copy-start | bytes 388
  0.0 12.3 %copy-start.1 = (bf16[2,2,32,80]{3,2,1,0:T(8,128)(2,1)S(1)}, bf16[2,2,32,80]{3,2,1,0:T(8,128)(2,1)}, u32[]{:S(2)}) copy-start(bf16[2,2,32,80]{3,2,1,0:T(8,128)(2,1)} %spec_ref.1) | copy-start | bytes 61444
  2.1 10.2 %collective-permute-start = (bf16[2,80,1408]{2,1,0:T(8,128)(2,1)S(1)}, bf16[2,80,1408]{2,1,0:T(8,128)(2,1)S(1)}, u32[]{:S(2)}, u32[]{:S(2)}) collective-permute-start(bf16[2,80,1408]{2,1,0:T(8,128)(2,1)S(1)} %fusion.1), channel_id=1, source_target_pairs={{0,1},{1,0},{2,3},{3,2},{4,5},{5,4},{6,7},{7,6},{8,9},{9,8},{10,11... | collective-permute-start | bytes 1351688 | tf_op jit(solution)/shard_map/ppermute | solution.py:365
  11.2 30.6 %copy-start.3 = (s32[2560]{0:T(1024)S(1)}, s32[2560]{0:T(1024)}, u32[]{:S(2)}) copy-start(s32[2560]{0:T(1024)} %refs_1_.1) | copy-start | bytes 30724
  11.2 30.6 %copy-start.4 = (bf16[32,32]{1,0:T(8,128)(2,1)S(1)}, bf16[32,32]{1,0:T(8,128)(2,1)}, u32[]{:S(2)}) copy-start(bf16[32,32]{1,0:T(8,128)(2,1)} %refs_2_.1) | copy-start | bytes 6148
  28.6 24.8 %all-to-all-start.1 = ((bf16[16,16,128]{2,1,0:T(8,128)(2,1)}), bf16[16,16,128]{2,1,0:T(8,128)(2,1)S(1)}, u32[]{:S(2)}, u32[]{:S(2)}) async-start(bf16[16,16,128]{2,1,0:T(8,128)(2,1)} %sums.1), calls=%async_computation.1 | async-start | bytes 131072 | tf_op jit(solution)/shard_map/all_to_all | solution.py:415
  85.4 6.6 %collective-permute-start.1 = (f32[2,2,32,80]{3,2,1,0:T(8,128)S(1)}, f32[2,2,32,80]{3,2,1,0:T(8,128)S(1)}, u32[]{:S(2)}, u32[]{:S(2)}) collective-permute-start(f32[2,2,32,80]{3,2,1,0:T(8,128)S(1)} %direct_other.1), channel_id=1, source_target_pairs={{0,1},{1,0},{2,3},{3,2},{4,5},{5,4},{6,7},{7,6},{8,9},{9,8},{10,11... | collective-permute-start | bytes 122888 | tf_op jit(solution)/shard_map/ppermute | solution.py:455

commit v5 on v4

--- a/solution.py
+++ b/solution.py
@@ -352,16 +352,17 @@
 
     deal_row = deal_list.reshape(1, waves)
     half = half_lat // 2
-    packed = jnp.concatenate(
-        [
-            jnp.where(lax.axis_index("lev") & 1 == 0, legendre[:, :, half:], legendre[:, :, :half]),
-            jnp.pad(
-                spec_in.reshape(slots, 2 * fields, cols),
-                ((0, 0), (0, cols - 2 * fields), (0, BLK - cols)),
-            ),
-        ],
-        axis=2,
-    )
+    zero = jnp.zeros((), BF16)
+    packed = jnp.where(
+        lax.axis_index("lev") & 1 == 0,
+        lax.pad(legendre, zero, ((0, 0, 0), (0, 0, 0), (-half, BLK, 0))),
+        lax.pad(legendre, zero, ((0, 0, 0), (0, 0, 0), (0, BLK - half, 0))),
+    )
+    tail = jnp.pad(
+        spec_in.reshape(slots, 2 * fields, cols),
+        ((0, 0), (0, cols - 2 * fields), (half, BLK - cols)),
+    )
+    packed = jnp.where(lax.broadcasted_iota(jnp.int32, (1, 1, half + BLK), 2) < half, packed, tail)
     packed = lax.ppermute(packed, "lev", pairs)
 
     table, turns, weights, mix, grams = pl.pallas_call(

time: 93 us -> 92.2 us (level)
  no operation moved by 1% of the time
where the time goes in v5:
time: 92.2 us; the launch traced here: 91.9 us
  blocking collectives  42.5 us (46%)
  starting transfers between devices  27.7 us (30%)
  waiting for transfers between devices  10.6 us (11%)
  Pallas kernels  8.91 us (10%)
  other arithmetic  2 us (2%)
    all_to_all x1, blocking collectives, local(): lax.all_to_all(partial_sums, 'lev', 0, 0, tiled=True, axis_index_groups=s...  14.9 us
    all_to_all x1, blocking collectives, local(): analysed = lax.all_to_all(analysed, 'lat', 0, 0, tiled=True)  14.4 us
    all_to_all x1, blocking collectives, local(): lax.all_to_all(copies, 'lev', 0, 0, tiled=True, axis_index_groups=same_core)  13.2 us
    all_to_all x1, starting transfers between devices, local(): fourier = lax.all_to_all(fourier, 'lat', 0, 0, tiled=True)  13.2 us
    all_to_all x1, waiting for transfers between devices, local(): fourier = lax.all_to_all(fourier, 'lat', 0, 0, tiled=True)  9.11 us
    ppermute x1, starting transfers between devices, local(): packed = lax.ppermute(packed, 'lev', pairs)  8.79 us
    ppermute x1, starting transfers between devices, local(): share = lax.ppermute(direct(False, other), 'lev', pairs)  5.69 us
    pallas_call x1, Pallas kernels, local(): pl.pallas_call(lambda *refs: grid_kernel((2.0 * waves) ** (-0.5), *refs),...  3.86 us
  transfers between devices with their start and end apart: 3, of which 3 were waited for; matrix products, arithmetic and copies ran while one was open for 0% of the time, Pallas kernels for 3%

profile of v5, /device:TPU:1, one launch (start us, length us, event | category | flops | bytes accessed | tf_op | source)
XLA Modules:
  0.0 91.9 jit_solution(9397598552526619690)
XLA Ops:
  0.0 0.0 copy-start
  0.0 0.0 copy-start.2
  0.0 0.0 copy-start.1
  0.0 1.4 %fusion.1 = bf16[2,80,1408]{2,1,0:T(8,128)(2,1)S(1)} fusion(bf16[2,80,2560]{2,1,0:T(8,128)(2,1)} %leg_ref.1, bf16[2,64,80]{2,1,0:T(8,128)(2,1)} %bitcast.2, pred[]{:T(512)S(6)} %eq.3, pred[1408]{0:T(1024)(128)(4,1)S(1)} %iota_compare_fusion), kind=kLoop, calls=%fused_computation.2 | loop fusion | flops 450560 | bytes 1754497 | tf_op jit(solution)/shard_map/jit(_where)/select_n | solution.py:365
  1.4 8.8 %collective-permute-start = (bf16[2,80,1408]{2,1,0:T(8,128)(2,1)S(1)}, bf16[2,80,1408]{2,1,0:T(8,128)(2,1)S(1)}, u32[]{:S(2)}, u32[]{:S(2)}) collective-permute-start(bf16[2,80,1408]{2,1,0:T(8,128)(2,1)S(1)} %fusion.1), channel_id=1, source_target_pairs={{0,1},{1,0},{2,3},{3,2},{4,5},{5,4},{6,7},{7,6},{8,9},{9,8},{10,11... | collective-permute-start | bytes 1351688 | tf_op jit(solution)/shard_map/ppermute | solution.py:366
  10.2 0.0 copy-done
  10.2 0.0 copy-done.2
  10.2 0.3 own.1.own_ref.refs_1_
  10.5 0.0 copy-start.3
  10.5 0.0 copy-start.4
  10.5 1.0 %collective-permute-done.packed_ref = bf16[2,80,1408]{2,1,0:T(8,128)(2,1)S(1)} collective-permute-done((bf16[2,80,1408]{2,1,0:T(8,128)(2,1)S(1)}, bf16[2,80,1408]{2,1,0:T(8,128)(2,1)S(1)}, u32[]{:S(2)}, u32[]{:S(2)}) %collective-permute-start) | collective-permute-done | bytes 450592 | tf_op jit(solution)/shard_map/ppermute | solution.py:366
  11.6 0.0 copy-done.1
  11.6 0.7 inverse.1
  12.3 14.9 %all_to_all.20.in_ref = bf16[16,160,128]{2,1,0:T(8,128)(2,1)S(1)} all-to-all(bf16[16,160,128]{2,1,0:T(8,128)(2,1)S(1)} %get-tuple-element.12), channel_id=1, replica_groups={{0,2,4,6,8,10,12,14,16,18,20,22,24,26,28,30},{1,3,5,7,9,11,13,15,17,19,..., dimensions={0} | all-to-all | bytes 1310720 | tf_op jit(solution)/shard_map/all_to_all | solution.py:404
  27.2 0.7 sums.1
  27.9 13.2 %all-to-all-start.1 = ((bf16[16,16,128]{2,1,0:T(8,128)(2,1)}), bf16[16,16,128]{2,1,0:T(8,128)(2,1)S(1)}, u32[]{:S(2)}, u32[]{:S(2)}) async-start(bf16[16,16,128]{2,1,0:T(8,128)(2,1)} %sums.1), calls=%async_computation.1 | async-start | bytes 131072 | tf_op jit(solution)/shard_map/all_to_all | solution.py:416
  41.1 0.0 copy-done.3
  41.1 0.0 copy-done.4
  41.1 2.4 %tables.1 = (bf16[64,10880]{1,0:T(8,128)(2,1)S(1)}, f32[4,32,128]{2,1,0:T(8,128)S(1)}, f32[8,128]{1,0:T(8,128)S(1)}, bf16[256,256]{1,0:T(8,128)(2,1)S(1)}, bf16[5,64,128]{2,1,0:T(8,128)(2,1)S(1)}) custom-call(s32[32]{0:T(128)S(1)} %copy-done.2, s32[2560]{0:T(1024)S(1)} %copy-done.3, bf16[32,32]{1,0:T(8,128)(2,1)S(1)} %copy-done.4), custom_call_target="tpu_custom_call" | custom-call | flops 20000000 | bytes 4000000 | tf_op jit(solution)/shard_map/tables/pallas_call | solution.py:368
  43.6 9.1 %all-to-all-done.1.refs_0_ = bf16[16,16,128]{2,1,0:T(8,128)(2,1)S(1)} async-done(((bf16[16,16,128]{2,1,0:T(8,128)(2,1)}), bf16[16,16,128]{2,1,0:T(8,128)(2,1)S(1)}, u32[]{:S(2)}, u32[]{:S(2)}) %all-to-all-start.1) | async-done | bytes 65568 | tf_op jit(solution)/shard_map/all_to_all | solution.py:416
  52.7 3.9 %grid_rows.1 = bf16[16,16,128]{2,1,0:T(8,128)(2,1)S(1)} custom-call(bf16[16,16,128]{2,1,0:T(8,128)(2,1)S(1)} %all-to-all-done.1.refs_0_, bf16[64,10880]{1,0:T(8,128)(2,1)S(1)} %get-tuple-element.13.refs_1_, f32[4,32,128]{2,1,0:T(8,128)S(1)} %get-tuple-element.14.refs_2_, f32[8,128]{1,0:T(8,128)S(1)} %get-tuple-element.15.refs_3_, ...), custom_call_target="tpu_custom_call" | custom-call | tf_op jit(solution)/shard_map/grid_rows/pallas_call | solution.py:417
  56.5 14.4 %all_to_all.21.in_ref = bf16[16,16,128]{2,1,0:T(8,128)(2,1)S(1)} all-to-all(bf16[16,16,128]{2,1,0:T(8,128)(2,1)S(1)} %grid_rows.1), channel_id=1, replica_groups=mesh['lat'=16,'lev'=32] {'lat'}, dimensions={0} | all-to-all | bytes 131072 | tf_op jit(solution)/shard_map/all_to_all | solution.py:431
  71.0 0.1 copies.1
  71.0 13.2 %all_to_all.22.refs_0_ = bf16[16,160,128]{2,1,0:T(8,128)(2,1)S(1)} all-to-all(bf16[16,160,128]{2,1,0:T(8,128)(2,1)S(1)} %copies.1), channel_id=1, replica_groups={{0,2,4,6,8,10,12,14,16,18,20,22,24,26,28,30},{1,3,5,7,9,11,13,15,17,19,..., dimensions={0} | all-to-all | bytes 1310720 | tf_op jit(solution)/shard_map/all_to_all | solution.py:441
  84.3 0.4 direct_other.1
  84.7 5.7 %collective-permute-start.1 = (f32[2,2,32,80]{3,2,1,0:T(8,128)S(1)}, f32[2,2,32,80]{3,2,1,0:T(8,128)S(1)}, u32[]{:S(2)}, u32[]{:S(2)}) collective-permute-start(f32[2,2,32,80]{3,2,1,0:T(8,128)S(1)} %direct_other.1), channel_id=1, source_target_pairs={{0,1},{1,0},{2,3},{3,2},{4,5},{5,4},{6,7},{7,6},{8,9},{9,8},{10,11... | collective-permute-start | bytes 122888 | tf_op jit(solution)/shard_map/ppermute | solution.py:456
  90.4 0.4 direct_own.1
  90.8 0.5 collective-permute-done.1
  91.3 0.6 add.7
  (1 shorter events, 0.0 us)
Async XLA Ops:
  0.0 10.2 %copy-start = (bf16[2,80,2560]{2,1,0:T(8,128)(2,1)S(1)}, bf16[2,80,2560]{2,1,0:T(8,128)(2,1)}, u32[]{:S(2)}) copy-start(bf16[2,80,2560]{2,1,0:T(8,128)(2,1)} %leg_ref.1) | copy-start | bytes 2457604
  0.0 10.2 %copy-start.2 = (s32[32]{0:T(128)S(1)}, s32[32]{0:T(128)}, u32[]{:S(2)}) copy-start(s32[32]{0:T(128)} %refs_0_.1) | copy-start | bytes 388
  0.0 11.6 %copy-start.1 = (bf16[2,2,32,80]{3,2,1,0:T(8,128)(2,1)S(1)}, bf16[2,2,32,80]{3,2,1,0:T(8,128)(2,1)}, u32[]{:S(2)}) copy-start(bf16[2,2,32,80]{3,2,1,0:T(8,128)(2,1)} %spec_ref.1) | copy-start | bytes 61444
  1.4 10.2 %collective-permute-start = (bf16[2,80,1408]{2,1,0:T(8,128)(2,1)S(1)}, bf16[2,80,1408]{2,1,0:T(8,128)(2,1)S(1)}, u32[]{:S(2)}, u32[]{:S(2)}) collective-permute-start(bf16[2,80,1408]{2,1,0:T(8,128)(2,1)S(1)} %fusion.1), channel_id=1, source_target_pairs={{0,1},{1,0},{2,3},{3,2},{4,5},{5,4},{6,7},{7,6},{8,9},{9,8},{10,11... | collective-permute-start | bytes 1351688 | tf_op jit(solution)/shard_map/ppermute | solution.py:366
  10.5 30.6 %copy-start.3 = (s32[2560]{0:T(1024)S(1)}, s32[2560]{0:T(1024)}, u32[]{:S(2)}) copy-start(s32[2560]{0:T(1024)} %refs_1_.1) | copy-start | bytes 30724
  10.5 30.6 %copy-start.4 = (bf16[32,32]{1,0:T(8,128)(2,1)S(1)}, bf16[32,32]{1,0:T(8,128)(2,1)}, u32[]{:S(2)}) copy-start(bf16[32,32]{1,0:T(8,128)(2,1)} %refs_2_.1) | copy-start | bytes 6148
  27.9 24.8 %all-to-all-start.1 = ((bf16[16,16,128]{2,1,0:T(8,128)(2,1)}), bf16[16,16,128]{2,1,0:T(8,128)(2,1)S(1)}, u32[]{:S(2)}, u32[]{:S(2)}) async-start(bf16[16,16,128]{2,1,0:T(8,128)(2,1)} %sums.1), calls=%async_computation.1 | async-start | bytes 131072 | tf_op jit(solution)/shard_map/all_to_all | solution.py:416
  84.7 6.6 %collective-permute-start.1 = (f32[2,2,32,80]{3,2,1,0:T(8,128)S(1)}, f32[2,2,32,80]{3,2,1,0:T(8,128)S(1)}, u32[]{:S(2)}, u32[]{:S(2)}) collective-permute-start(f32[2,2,32,80]{3,2,1,0:T(8,128)S(1)} %direct_other.1), channel_id=1, source_target_pairs={{0,1},{1,0},{2,3},{3,2},{4,5},{5,4},{6,7},{7,6},{8,9},{9,8},{10,11... | collective-permute-start | bytes 122888 | tf_op jit(solution)/shard_map/ppermute | solution.py:456

commit v6 on v5

--- a/solution.py
+++ b/solution.py
@@ -353,10 +353,10 @@
     deal_row = deal_list.reshape(1, waves)
     half = half_lat // 2
     zero = jnp.zeros((), BF16)
-    packed = jnp.where(
-        lax.axis_index("lev") & 1 == 0,
-        lax.pad(legendre, zero, ((0, 0, 0), (0, 0, 0), (-half, BLK, 0))),
-        lax.pad(legendre, zero, ((0, 0, 0), (0, 0, 0), (0, BLK - half, 0))),
+    packed = lax.dynamic_slice(
+        lax.pad(legendre, zero, ((0, 0, 0), (0, 0, 0), (0, BLK, 0))),
+        (0, 0, half * (1 - (lax.axis_index("lev") & 1))),
+        (slots, cols, half + BLK),
     )
     tail = jnp.pad(
         spec_in.reshape(slots, 2 * fields, cols),

time: 92.2 us -> 92 us (level)
  no operation moved by 1% of the time
where the time goes in v6:
time: 92 us; the launch traced here: 91.7 us
  blocking collectives  42.5 us (46%)
  starting transfers between devices  27.7 us (30%)
  waiting for transfers between devices  9.97 us (11%)
  Pallas kernels  8.9 us (10%)
  other arithmetic  1.83 us (2%)
    all_to_all x1, blocking collectives, local(): lax.all_to_all(partial_sums, 'lev', 0, 0, tiled=True, axis_index_groups=s...  14.9 us
    all_to_all x1, blocking collectives, local(): analysed = lax.all_to_all(analysed, 'lat', 0, 0, tiled=True)  14.4 us
    all_to_all x1, blocking collectives, local(): lax.all_to_all(copies, 'lev', 0, 0, tiled=True, axis_index_groups=same_core)  13.2 us
    all_to_all x1, starting transfers between devices, local(): fourier = lax.all_to_all(fourier, 'lat', 0, 0, tiled=True)  13.2 us
    all_to_all x1, waiting for transfers between devices, local(): fourier = lax.all_to_all(fourier, 'lat', 0, 0, tiled=True)  9.1 us
    ppermute x1, starting transfers between devices, local(): packed = lax.ppermute(packed, 'lev', pairs)  8.77 us
    ppermute x1, starting transfers between devices, local(): share = lax.ppermute(direct(False, other), 'lev', pairs)  5.69 us
    pallas_call x1, Pallas kernels, local(): pl.pallas_call(lambda *refs: grid_kernel((2.0 * waves) ** (-0.5), *refs),...  3.86 us
  transfers between devices with their start and end apart: 3, of which 3 were waited for; matrix products, arithmetic and copies ran while one was open for 0% of the time, Pallas kernels for 3%

profile of v6, /device:TPU:1, one launch (start us, length us, event | category | flops | bytes accessed | tf_op | source)
XLA Modules:
  0.0 91.7 jit_solution(14941619331812337640)
XLA Ops:
  0.0 0.0 copy-start
  0.0 0.0 copy-start.1
  0.0 1.2 %fusion = bf16[2,80,1408]{2,1,0:T(8,128)(2,1)S(1)} fusion(s32[]{:T(128)S(6)} %select_n.7, bf16[2,80,2560]{2,1,0:T(8,128)(2,1)} %leg_ref.1, bf16[2,64,80]{2,1,0:T(8,128)(2,1)} %bitcast.2, pred[1408]{0:T(1024)(128)(4,1)S(1)} %iota_compare_fusion), kind=kLoop, calls=%fused_computation.1 | loop fusion | flops 225280 | bytes 1291652 | tf_op jit(solution)/shard_map/jit(_where)/select_n | solution.py:365
  1.2 8.8 %collective-permute-start = (bf16[2,80,1408]{2,1,0:T(8,128)(2,1)S(1)}, bf16[2,80,1408]{2,1,0:T(8,128)(2,1)S(1)}, u32[]{:S(2)}, u32[]{:S(2)}) collective-permute-start(bf16[2,80,1408]{2,1,0:T(8,128)(2,1)S(1)} %fusion), channel_id=1, source_target_pairs={{0,1},{1,0},{2,3},{3,2},{4,5},{5,4},{6,7},{7,6},{8,9},{9,8},{10,11... | collective-permute-start | bytes 1351688 | tf_op jit(solution)/shard_map/ppermute | solution.py:366
  10.0 0.0 copy-done
  10.0 0.0 copy-start.2
  10.0 0.6 copy-done.2
  10.7 0.3 own.1.own_ref.refs_1_
  11.0 0.0 copy-start.3
  11.0 0.0 copy-start.4
  11.0 0.0 copy-start.5
  11.0 0.4 collective-permute-done.packed_ref
  11.4 0.0 copy-done.1
  11.4 0.7 inverse.1
  12.1 14.9 %all_to_all.20.in_ref = bf16[16,160,128]{2,1,0:T(8,128)(2,1)S(1)} all-to-all(bf16[16,160,128]{2,1,0:T(8,128)(2,1)S(1)} %get-tuple-element.12), channel_id=1, replica_groups={{0,2,4,6,8,10,12,14,16,18,20,22,24,26,28,30},{1,3,5,7,9,11,13,15,17,19,..., dimensions={0} | all-to-all | bytes 1310720 | tf_op jit(solution)/shard_map/all_to_all | solution.py:404
  27.0 0.7 sums.1
  27.7 13.2 %all-to-all-start.1 = ((bf16[16,16,128]{2,1,0:T(8,128)(2,1)}), bf16[16,16,128]{2,1,0:T(8,128)(2,1)S(1)}, u32[]{:S(2)}, u32[]{:S(2)}) async-start(bf16[16,16,128]{2,1,0:T(8,128)(2,1)} %sums.1), calls=%async_computation.1 | async-start | bytes 131072 | tf_op jit(solution)/shard_map/all_to_all | solution.py:416
  40.9 0.0 copy-done.3
  40.9 0.0 copy-done.4
  40.9 0.0 copy-done.5
  40.9 2.4 %tables.1 = (bf16[64,10880]{1,0:T(8,128)(2,1)S(1)}, f32[4,32,128]{2,1,0:T(8,128)S(1)}, f32[8,128]{1,0:T(8,128)S(1)}, bf16[256,256]{1,0:T(8,128)(2,1)S(1)}, bf16[5,64,128]{2,1,0:T(8,128)(2,1)S(1)}) custom-call(s32[32]{0:T(128)S(1)} %copy-done.3, s32[2560]{0:T(1024)S(1)} %copy-done.4, bf16[32,32]{1,0:T(8,128)(2,1)S(1)} %copy-done.5), custom_call_target="tpu_custom_call" | custom-call | flops 20000000 | bytes 4000000 | tf_op jit(solution)/shard_map/tables/pallas_call | solution.py:368
  43.4 9.1 %all-to-all-done.1.refs_0_ = bf16[16,16,128]{2,1,0:T(8,128)(2,1)S(1)} async-done(((bf16[16,16,128]{2,1,0:T(8,128)(2,1)}), bf16[16,16,128]{2,1,0:T(8,128)(2,1)S(1)}, u32[]{:S(2)}, u32[]{:S(2)}) %all-to-all-start.1) | async-done | bytes 65568 | tf_op jit(solution)/shard_map/all_to_all | solution.py:416
  52.5 3.9 %grid_rows.1 = bf16[16,16,128]{2,1,0:T(8,128)(2,1)S(1)} custom-call(bf16[16,16,128]{2,1,0:T(8,128)(2,1)S(1)} %all-to-all-done.1.refs_0_, bf16[64,10880]{1,0:T(8,128)(2,1)S(1)} %get-tuple-element.13.refs_1_, f32[4,32,128]{2,1,0:T(8,128)S(1)} %get-tuple-element.14.refs_2_, f32[8,128]{1,0:T(8,128)S(1)} %get-tuple-element.15.refs_3_, ...), custom_call_target="tpu_custom_call" | custom-call | tf_op jit(solution)/shard_map/grid_rows/pallas_call | solution.py:417
  56.3 14.4 %all_to_all.21.in_ref = bf16[16,16,128]{2,1,0:T(8,128)(2,1)S(1)} all-to-all(bf16[16,16,128]{2,1,0:T(8,128)(2,1)S(1)} %grid_rows.1), channel_id=1, replica_groups=mesh['lat'=16,'lev'=32] {'lat'}, dimensions={0} | all-to-all | bytes 131072 | tf_op jit(solution)/shard_map/all_to_all | solution.py:431
  70.8 0.1 copies.1
  70.8 13.2 %all_to_all.22.refs_0_ = bf16[16,160,128]{2,1,0:T(8,128)(2,1)S(1)} all-to-all(bf16[16,160,128]{2,1,0:T(8,128)(2,1)S(1)} %copies.1), channel_id=1, replica_groups={{0,2,4,6,8,10,12,14,16,18,20,22,24,26,28,30},{1,3,5,7,9,11,13,15,17,19,..., dimensions={0} | all-to-all | bytes 1310720 | tf_op jit(solution)/shard_map/all_to_all | solution.py:441
  84.1 0.4 direct_other.1
  84.5 5.7 %collective-permute-start.1 = (f32[2,2,32,80]{3,2,1,0:T(8,128)S(1)}, f32[2,2,32,80]{3,2,1,0:T(8,128)S(1)}, u32[]{:S(2)}, u32[]{:S(2)}) collective-permute-start(f32[2,2,32,80]{3,2,1,0:T(8,128)S(1)} %direct_other.1), channel_id=1, source_target_pairs={{0,1},{1,0},{2,3},{3,2},{4,5},{5,4},{6,7},{7,6},{8,9},{9,8},{10,11... | collective-permute-start | bytes 122888 | tf_op jit(solution)/shard_map/ppermute | solution.py:456
  90.2 0.4 direct_own.1
  90.6 0.5 collective-permute-done.1
  91.1 0.6 add.11
  (1 shorter events, 0.0 us)
Async XLA Ops:
  0.0 10.0 %copy-start = (bf16[2,80,2560]{2,1,0:T(8,128)(2,1)S(1)}, bf16[2,80,2560]{2,1,0:T(8,128)(2,1)}, u32[]{:S(2)}) copy-start(bf16[2,80,2560]{2,1,0:T(8,128)(2,1)} %leg_ref.1) | copy-start | bytes 2457604
  0.0 11.4 %copy-start.1 = (bf16[2,2,32,80]{3,2,1,0:T(8,128)(2,1)S(1)}, bf16[2,2,32,80]{3,2,1,0:T(8,128)(2,1)}, u32[]{:S(2)}) copy-start(bf16[2,2,32,80]{3,2,1,0:T(8,128)(2,1)} %spec_ref.1) | copy-start | bytes 61444
  1.2 10.2 %collective-permute-start = (bf16[2,80,1408]{2,1,0:T(8,128)(2,1)S(1)}, bf16[2,80,1408]{2,1,0:T(8,128)(2,1)S(1)}, u32[]{:S(2)}, u32[]{:S(2)}) collective-permute-start(bf16[2,80,1408]{2,1,0:T(8,128)(2,1)S(1)} %fusion), channel_id=1, source_target_pairs={{0,1},{1,0},{2,3},{3,2},{4,5},{5,4},{6,7},{7,6},{8,9},{9,8},{10,11... | collective-permute-start | bytes 1351688 | tf_op jit(solution)/shard_map/ppermute | solution.py:366
  10.0 0.7 copy-start.2
  11.0 29.9 %copy-start.3 = (s32[32]{0:T(128)S(1)}, s32[32]{0:T(128)}, u32[]{:S(2)}) copy-start(s32[32]{0:T(128)} %refs_0_.1) | copy-start | bytes 388
  11.0 29.9 %copy-start.4 = (s32[2560]{0:T(1024)S(1)}, s32[2560]{0:T(1024)}, u32[]{:S(2)}) copy-start(s32[2560]{0:T(1024)} %refs_1_.1) | copy-start | bytes 30724
  11.0 29.9 %copy-start.5 = (bf16[32,32]{1,0:T(8,128)(2,1)S(1)}, bf16[32,32]{1,0:T(8,128)(2,1)}, u32[]{:S(2)}) copy-start(bf16[32,32]{1,0:T(8,128)(2,1)} %refs_2_.1) | copy-start | bytes 6148
  27.7 24.8 %all-to-all-start.1 = ((bf16[16,16,128]{2,1,0:T(8,128)(2,1)}), bf16[16,16,128]{2,1,0:T(8,128)(2,1)S(1)}, u32[]{:S(2)}, u32[]{:S(2)}) async-start(bf16[16,16,128]{2,1,0:T(8,128)(2,1)} %sums.1), calls=%async_computation.1 | async-start | bytes 131072 | tf_op jit(solution)/shard_map/all_to_all | solution.py:416
  84.5 6.6 %collective-permute-start.1 = (f32[2,2,32,80]{3,2,1,0:T(8,128)S(1)}, f32[2,2,32,80]{3,2,1,0:T(8,128)S(1)}, u32[]{:S(2)}, u32[]{:S(2)}) collective-permute-start(f32[2,2,32,80]{3,2,1,0:T(8,128)S(1)} %direct_other.1), channel_id=1, source_target_pairs={{0,1},{1,0},{2,3},{3,2},{4,5},{5,4},{6,7},{7,6},{8,9},{9,8},{10,11... | collective-permute-start | bytes 122888 | tf_op jit(solution)/shard_map/ppermute | solution.py:456

commit v7 on v6

--- a/solution.py
+++ b/solution.py
@@ -13,12 +13,17 @@
 F32 = jnp.float32
 BF16 = jnp.bfloat16
 VMEM = pl.BlockSpec(memory_space=pltpu.VMEM)
-SMEM = pl.BlockSpec(memory_space=pltpu.SMEM)
 NT = (((1,), (1,)), ((), ()))
 
 
 def params(kib=16384):
     return pltpu.CompilerParams(vmem_limit_bytes=kib * 1024)
+
+
+def rows_block(core, fifth, fifths):
+    if fifth == fifths - 1:
+        return 2 * fifths - 1 - core
+    return core * (fifths - 1) + fifth
 
 
 def wave_of(deal_ref, slot):
@@ -73,7 +78,7 @@
             for half in range(2):
                 begin = (2 * fifth + half) * BLK
                 value = packed_ref[slot, :, begin : begin + BLK]
-                row_block = 2 * fifths * core + 2 * fifth + half
+                row_block = 2 * rows_block(core, fifth, fifths) + half
                 parts.append(mask_rows(value, wave, live, row_block, 4 * fifths))
             other_right = jnp.concatenate(parts, axis=1)
             here = slice(fifth * 2 * BLK, (fifth + 1) * 2 * BLK)
@@ -139,41 +144,47 @@
 
 
 def widths(core, fifths):
-    return [2 * BLK * (core * fifths + fifth + 1) for fifth in range(fifths)]
-
-
-def own_kernel(deal_ref, leg_ref, own_ref):
+    return [2 * BLK * (rows_block(core, fifth, fifths) + 1) for fifth in range(fifths)]
+
+
+def own_rows(deal_ref, leg_ref, own_ref):
     lat, lev = lax.axis_index("lat"), lax.axis_index("lev")
     core = lax.rem(lev, 2)
     slots, cols, half_rows = own_ref.shape
     blocks = half_rows // BLK
+    fifths = blocks // 2
     for slot in range(slots):
         wave = wave_of(deal_ref, slots * lat + slot)
         live = live_degrees(wave, lev * cols, (cols, BLK))
         for block in range(blocks):
-            row_block = blocks * core + block
+            row_block = 2 * rows_block(core, block // 2, fifths) + block % 2
             value = leg_ref[slot, :, pl.ds(pl.multiple_of(row_block * BLK, BLK), BLK)]
             own_ref[slot, :, block * BLK : (block + 1) * BLK] = mask_rows(
                 value, wave, live, row_block, 2 * blocks
             )
 
 
-def table_kernel(fifths, deal_ref, lengths_ref, mixing_ref,
-                 table_ref, turn_ref, weight_ref, mix_ref, gram_ref):
+def table_kernel(fifths, deal_ref, lengths_ref, mixing_ref, leg_ref,
+                 own_ref, table_ref, turn_ref, weight_ref, mix_ref, gram_ref):
     lat, lev = lax.axis_index("lat"), lax.axis_index("lev")
     core = lax.rem(lev, 2)
-    half_lat = lengths_ref.shape[0]
+    half_lat = lengths_ref.shape[0] * BLK
     half_rows = half_lat // 2
-    waves = deal_ref.shape[0]
+    waves = deal_ref.shape[1]
+    own_rows(deal_ref, leg_ref, own_ref)
     fields = mixing_ref.shape[0]
     shape = (waves, BLK)
     sub = lax.broadcasted_iota(jnp.int32, shape, 0)
     lane = lax.broadcasted_iota(jnp.int32, shape, 1)
     lane_f = lane.astype(F32)
-    wave = jnp.zeros(shape, jnp.int32)
-    for slot in range(waves):
-        wave = jnp.where(sub == slot, deal_ref[slot], wave)
-    wave_f = wave.astype(F32)
+    square = (waves, waves)
+    diagonal = lax.broadcasted_iota(jnp.int32, square, 0) == lax.broadcasted_iota(jnp.int32, square, 1)
+    wave_f = jnp.where(diagonal, jnp.broadcast_to(deal_ref[...], square), 0).astype(F32)
+    wave_f = jnp.broadcast_to(jnp.sum(wave_f, axis=1, keepdims=True), shape)
+    wave = wave_f.astype(jnp.int32)
+    lengths = lengths_ref[...]
+    position = lax.broadcasted_iota(jnp.int32, lengths.shape, 0) * BLK
+    position = position + lax.broadcasted_iota(jnp.int32, lengths.shape, 1)
     for pair in range(2):
         quarter = 2 * pair + (lane >= BLK // 2).astype(jnp.int32)
         turn = lax.rem(quarter * wave, 4)
@@ -193,19 +204,20 @@
     mix_ref[...] = jnp.where(same, wide, 0.0).astype(BF16)
     weight_ref[...] = jnp.zeros_like(weight_ref)
     group = half_rows // fifths
-    first_row = core * half_rows + (lev // 2) * (2 * BLK // CHIPS) + lat
+    first_row = (lev // 2) * (group // CHIPS) + lat
 
     def build(which):
         main = widths(which, fifths)
         extra = sum(main)
         start = 0
-        beyond = 0
+        beyond = jnp.zeros((1, 1), F32)
         for fifth, width in enumerate(main):
-            row = first_row + fifth * group
-            length = lengths_ref[row]
-            points = length // 4
-            beyond = jnp.maximum(beyond, points - width)
-            length_f = jnp.full(shape, length, jnp.int32).astype(F32)
+            row = first_row + rows_block(which, fifth, fifths) * group
+            length_f = jnp.where(position == row, lengths, 0).astype(F32)
+            length_f = jnp.sum(jnp.sum(length_f, axis=0, keepdims=True), axis=1, keepdims=True)
+            beyond = jnp.maximum(beyond, length_f * 0.25 - float(width))
+            length_f = jnp.broadcast_to(length_f, shape)
+            points = length_f * 0.25
             low_cos, low_sin = circle(wave_f * lane_f, length_f)
             high_cos, high_sin = circle(wave_f * lane_f * float(BLK), length_f)
             blocks = width // BLK
@@ -214,16 +226,19 @@
                 a_sin = jnp.broadcast_to(high_sin[:, block : block + 1], shape)
                 cosine = a_cos * low_cos - a_sin * low_sin
                 sine = a_sin * low_cos + a_cos * low_sin
-                inside = lane + block * BLK < points
+                inside = lane_f + float(block * BLK) < points
                 begin = start + block * BLK if block < blocks else extra + fifth * BLK
                 here = slice(begin, begin + BLK)
-                table_ref[0:waves, here] = jnp.where(inside, cosine, 0.0).astype(BF16)
-                table_ref[waves : 2 * waves, here] = jnp.where(inside, -sine, 0.0).astype(BF16)
+                if block >= rows_block(which, fifth, fifths):
+                    cosine = jnp.where(inside, cosine, 0.0)
+                    sine = jnp.where(inside, sine, 0.0)
+                table_ref[0:waves, here] = cosine.astype(BF16)
+                table_ref[waves : 2 * waves, here] = (-sine).astype(BF16)
             row_f = jnp.full((1, BLK), row, jnp.int32).astype(F32) + 0.5
             _, sine = circle(row_f, jnp.full((1, BLK), 4.0 * half_lat, F32))
             weight_ref[fifth : fifth + 1, :] = sine / jnp.sqrt(length_f[0:1, :])
             start += width
-        weight_ref[fifths : fifths + 1, :] = jnp.full((1, BLK), beyond, jnp.int32).astype(F32)
+        weight_ref[fifths : fifths + 1, :] = jnp.broadcast_to(beyond, (1, BLK))
         start = 0
         for fifth, width in enumerate(main):
             table = table_ref[:, start : start + width]
@@ -352,43 +367,44 @@
 
     deal_row = deal_list.reshape(1, waves)
     half = half_lat // 2
+    other_core = 1 - (lax.axis_index("lev") & 1)
     zero = jnp.zeros((), BF16)
-    packed = lax.dynamic_slice(
-        lax.pad(legendre, zero, ((0, 0, 0), (0, 0, 0), (0, BLK, 0))),
-        (0, 0, half * (1 - (lax.axis_index("lev") & 1))),
-        (slots, cols, half + BLK),
-    )
+    group = half // fifths
+    first = half - group
+    padded = lax.pad(legendre, zero, ((0, 0, 0), (0, 0, 0), (0, half, 0)))
+    size = (slots, cols, half + BLK)
+    lanes = lax.broadcasted_iota(jnp.int32, (1, 1, half + BLK), 2)
     tail = jnp.pad(
         spec_in.reshape(slots, 2 * fields, cols),
         ((0, 0), (0, cols - 2 * fields), (half, BLK - cols)),
     )
-    packed = jnp.where(lax.broadcasted_iota(jnp.int32, (1, 1, half + BLK), 2) < half, packed, tail)
+    packed = jnp.where(
+        lanes < half,
+        jnp.where(
+            lanes < first,
+            lax.dynamic_slice(padded, (0, 0, first * other_core), size),
+            lax.dynamic_slice(padded, (0, 0, half_lat - half - group * other_core), size),
+        ),
+        tail,
+    )
     packed = lax.ppermute(packed, "lev", pairs)
 
-    table, turns, weights, mix, grams = pl.pallas_call(
+    own, table, turns, weights, mix, grams = pl.pallas_call(
         lambda *refs: table_kernel(fifths, *refs),
         out_shape=(
+            jax.ShapeDtypeStruct((slots, cols, fifths * 2 * BLK), BF16),
             jax.ShapeDtypeStruct((2 * waves, sum(widths(1, fifths)) + fifths * BLK), BF16),
             jax.ShapeDtypeStruct((4, waves, BLK), F32),
             jax.ShapeDtypeStruct((8, BLK), F32),
             jax.ShapeDtypeStruct((8 * fields, 8 * fields), BF16),
             jax.ShapeDtypeStruct((fifths, 2 * waves, BLK), BF16),
         ),
-        in_specs=[SMEM, SMEM, VMEM],
-        out_specs=(VMEM,) * 5,
+        in_specs=[VMEM] * 4,
+        out_specs=(VMEM,) * 6,
         compiler_params=params(),
         cost_estimate=pl.CostEstimate(flops=20_000_000, bytes_accessed=4_000_000, transcendentals=0),
         name="tables",
-    )(deal_list, circle_lengths, mixing)
-    own = pl.pallas_call(
-        own_kernel,
-        out_shape=jax.ShapeDtypeStruct((slots, cols, fifths * 2 * BLK), BF16),
-        in_specs=[VMEM, VMEM],
-        out_specs=VMEM,
-        compiler_params=params(),
-        cost_estimate=pl.CostEstimate(flops=1_000_000, bytes_accessed=1_300_000, transcendentals=0),
-        name="own",
-    )(deal_row, legendre)
+    )(deal_row, circle_lengths.reshape(-1, BLK), mixing, legendre)
 
     partial_sums, other = pl.pallas_call(
         inverse_kernel,

time: 92 us -> 92.5 us (level)
  blocking collectives: 42.5 us -> 67.6 us
  starting transfers between devices: 27.7 us -> 14.6 us
  waiting for transfers between devices: 9.97 us -> 0.47 us
  Pallas kernels: 8.9 us -> 7.29 us
    all_to_all x0 -> x1, blocking collectives: none -> 24.7 us  [local(): fourier = lax.all_to_all(fourier, 'lat', 0, 0, tiled=True)]
    all_to_all x1 -> x0, starting transfers between devices: 13.2 us -> none  [local(): fourier = lax.all_to_all(fourier, 'lat', 0, 0, tiled=True)]
    all_to_all x1 -> x0, waiting for transfers between devices: 9.1 us -> none  [local(): fourier = lax.all_to_all(fourier, 'lat', 0, 0, tiled=True)]
  transfers between devices with their start and end apart: 3 -> 2, of which waited for: 3 -> 1; matrix products, arithmetic and copies ran while one was open for 0% -> 0% of each run, Pallas kernels for 3% -> 3%
where the time goes in v7:
time: 92.5 us; the launch traced here: 92.2 us
  blocking collectives  67.6 us (73%)
  starting transfers between devices  14.6 us (16%)
  Pallas kernels  7.29 us (8%)
  other arithmetic  2.07 us (2%)
    all_to_all x1, blocking collectives, local(): fourier = lax.all_to_all(fourier, 'lat', 0, 0, tiled=True)  24.7 us
    all_to_all x1, blocking collectives, local(): lax.all_to_all(partial_sums, 'lev', 0, 0, tiled=True, axis_index_groups=s...  15.7 us
    all_to_all x1, blocking collectives, local(): analysed = lax.all_to_all(analysed, 'lat', 0, 0, tiled=True)  14.4 us
    all_to_all x1, blocking collectives, local(): lax.all_to_all(copies, 'lev', 0, 0, tiled=True, axis_index_groups=same_core)  12.9 us
    ppermute x1, starting transfers between devices, local(): packed = lax.ppermute(packed, 'lev', pairs)  8.78 us
    ppermute x1, starting transfers between devices, local(): share = lax.ppermute(direct(False, other), 'lev', pairs)  5.82 us
    pallas_call x1, Pallas kernels, local(): pl.pallas_call(lambda *refs: grid_kernel((2.0 * waves) ** (-0.5), *refs),...  3.5 us
    pallas_call x1, Pallas kernels, local(): pl.pallas_call(lambda *refs: table_kernel(fifths, *refs), out_shape=(jax....  2.08 us
  transfers between devices with their start and end apart: 2, of which 1 were waited for; matrix products, arithmetic and copies ran while one was open for 0% of the time, Pallas kernels for 3%

profile of v7, /device:TPU:1, one launch (start us, length us, event | category | flops | bytes accessed | tf_op | source)
XLA Modules:
  0.0 92.2 jit_solution(15703533696888457283)
XLA Ops:
  0.0 0.0 copy-start
  0.0 0.0 copy-start.1
  0.0 0.0 copy-start.3
  0.0 0.0 copy-start.2
  0.0 0.0 copy-start.4
  0.1 1.4 %fusion.1 = bf16[2,80,1408]{2,1,0:T(8,128)(2,1)S(1)} fusion(s32[]{:T(128)S(6)} %select_n.13, bf16[2,80,2560]{2,1,0:T(8,128)(2,1)} %refs_3_.1, s32[]{:T(128)S(6)} %select_n.14, bf16[2,64,80]{2,1,0:T(8,128)(2,1)} %bitcast.3, pred[1408]{0:T(1024)(128)(4,1)S(1)} %get-tuple-element.21, pred[1408]{0:T(1024)(128)(4,1)S(1)} %get-tuple-element.22), kind=kLoop, calls=%fused_computation.3 | loop fusion | flops 450560 | bytes 1293064 | tf_op jit(solution)/shard_map/jit(_where)/select_n | solution.py:381
  1.5 8.8 %collective-permute-start = (bf16[2,80,1408]{2,1,0:T(8,128)(2,1)S(1)}, bf16[2,80,1408]{2,1,0:T(8,128)(2,1)S(1)}, u32[]{:S(2)}, u32[]{:S(2)}) collective-permute-start(bf16[2,80,1408]{2,1,0:T(8,128)(2,1)S(1)} %fusion.1), channel_id=1, source_target_pairs={{0,1},{1,0},{2,3},{3,2},{4,5},{5,4},{6,7},{7,6},{8,9},{9,8},{10,11... | collective-permute-start | bytes 1351688 | tf_op jit(solution)/shard_map/ppermute | solution.py:390
  10.3 0.0 copy-done
  10.3 0.0 copy-done.3
  10.3 0.0 copy-done.2
  10.3 0.0 copy-done.4
  10.3 2.1 %tables.1 = (bf16[2,80,1280]{2,1,0:T(8,128)(2,1)S(1)}, bf16[64,9600]{1,0:T(8,128)(2,1)S(1)}, f32[4,32,128]{2,1,0:T(8,128)S(1)}, f32[8,128]{1,0:T(8,128)S(1)}, bf...) custom-call(s32[1,32]{1,0:T(1,128)S(1)} %bitcast.5, s32[20,128]{1,0:T(8,128)S(1)} %bitcast.4, ...), custom_call_target="tpu_custom_call" | custom-call | flops 20000000 | bytes 4000000 | tf_op jit(solution)/shard_map/tables/pallas_call | solution.py:392
  12.4 0.0 collective-permute-done.packed_ref
  12.4 0.0 copy-done.1
  12.4 0.7 inverse.1
  13.1 15.7 %all_to_all.20.in_ref = bf16[16,160,128]{2,1,0:T(8,128)(2,1)S(1)} all-to-all(bf16[16,160,128]{2,1,0:T(8,128)(2,1)S(1)} %get-tuple-element.14), channel_id=1, replica_groups={{0,2,4,6,8,10,12,14,16,18,20,22,24,26,28,30},{1,3,5,7,9,11,13,15,17,19,..., dimensions={0} | all-to-all | bytes 1310720 | tf_op jit(solution)/shard_map/all_to_all | solution.py:420
  28.8 0.1 sums.1
  28.9 24.7 %all_to_all.21.refs_0_ = bf16[16,16,128]{2,1,0:T(8,128)(2,1)S(1)} all-to-all(bf16[16,16,128]{2,1,0:T(8,128)(2,1)S(1)} %sums.1), channel_id=1, replica_groups=mesh['lat'=16,'lev'=32] {'lat'}, dimensions={0} | all-to-all | bytes 131072 | tf_op jit(solution)/shard_map/all_to_all | solution.py:432
  53.6 3.5 %grid_rows.1 = bf16[16,16,128]{2,1,0:T(8,128)(2,1)S(1)} custom-call(bf16[16,16,128]{2,1,0:T(8,128)(2,1)S(1)} %all_to_all.21.refs_0_, bf16[64,9600]{1,0:T(8,128)(2,1)S(1)} %get-tuple-element.15.refs_1_, f32[4,32,128]{2,1,0:T(8,128)S(1)} %get-tuple-element.16.refs_2_, f32[8,128]{1,0:T(8,128)S(1)} %get-tuple-element.17.refs_3_, ...), custom_call_target="tpu_custom_call" | custom-call | tf_op jit(solution)/shard_map/grid_rows/pallas_call | solution.py:433
  57.1 14.4 %all_to_all.22.in_ref = bf16[16,16,128]{2,1,0:T(8,128)(2,1)S(1)} all-to-all(bf16[16,16,128]{2,1,0:T(8,128)(2,1)S(1)} %grid_rows.1), channel_id=1, replica_groups=mesh['lat'=16,'lev'=32] {'lat'}, dimensions={0} | all-to-all | bytes 131072 | tf_op jit(solution)/shard_map/all_to_all | solution.py:447
  71.5 0.1 copies.1
  71.6 12.9 %all_to_all.23.refs_0_ = bf16[16,160,128]{2,1,0:T(8,128)(2,1)S(1)} all-to-all(bf16[16,160,128]{2,1,0:T(8,128)(2,1)S(1)} %copies.1), channel_id=1, replica_groups={{0,2,4,6,8,10,12,14,16,18,20,22,24,26,28,30},{1,3,5,7,9,11,13,15,17,19,..., dimensions={0} | all-to-all | bytes 1310720 | tf_op jit(solution)/shard_map/all_to_all | solution.py:457
  84.4 0.4 direct_other.1
  84.8 5.8 %collective-permute-start.1 = (f32[2,2,32,80]{3,2,1,0:T(8,128)S(1)}, f32[2,2,32,80]{3,2,1,0:T(8,128)S(1)}, u32[]{:S(2)}, u32[]{:S(2)}) collective-permute-start(f32[2,2,32,80]{3,2,1,0:T(8,128)S(1)} %direct_other.1), channel_id=1, source_target_pairs={{0,1},{1,0},{2,3},{3,2},{4,5},{5,4},{6,7},{7,6},{8,9},{9,8},{10,11... | collective-permute-start | bytes 122888 | tf_op jit(solution)/shard_map/ppermute | solution.py:472
  90.7 0.4 direct_own.1
  91.1 0.5 collective-permute-done.1
  91.5 0.6 add.16
  (1 shorter events, 0.0 us)
Async XLA Ops:
  0.0 10.3 %copy-start = (bf16[2,80,2560]{2,1,0:T(8,128)(2,1)S(1)}, bf16[2,80,2560]{2,1,0:T(8,128)(2,1)}, u32[]{:S(2)}) copy-start(bf16[2,80,2560]{2,1,0:T(8,128)(2,1)} %refs_3_.1) | copy-start | bytes 2457604
  0.0 12.4 %copy-start.1 = (bf16[2,2,32,80]{3,2,1,0:T(8,128)(2,1)S(1)}, bf16[2,2,32,80]{3,2,1,0:T(8,128)(2,1)}, u32[]{:S(2)}) copy-start(bf16[2,2,32,80]{3,2,1,0:T(8,128)(2,1)} %spec_ref.1) | copy-start | bytes 61444
  0.0 10.3 %copy-start.3 = (bf16[32,32]{1,0:T(8,128)(2,1)S(1)}, bf16[32,32]{1,0:T(8,128)(2,1)}, u32[]{:S(2)}) copy-start(bf16[32,32]{1,0:T(8,128)(2,1)} %refs_2_.1) | copy-start | bytes 6148
  0.0 10.3 %copy-start.2 = (s32[2560]{0:T(1024)S(1)}, s32[2560]{0:T(1024)}, u32[]{:S(2)}) copy-start(s32[2560]{0:T(1024)} %param.9) | copy-start | bytes 30724
  0.0 10.3 %copy-start.4 = (s32[32]{0:T(128)S(1)}, s32[32]{0:T(128)}, u32[]{:S(2)}) copy-start(s32[32]{0:T(128)} %param.8) | copy-start | bytes 388
  1.5 10.9 %collective-permute-start = (bf16[2,80,1408]{2,1,0:T(8,128)(2,1)S(1)}, bf16[2,80,1408]{2,1,0:T(8,128)(2,1)S(1)}, u32[]{:S(2)}, u32[]{:S(2)}) collective-permute-start(bf16[2,80,1408]{2,1,0:T(8,128)(2,1)S(1)} %fusion.1), channel_id=1, source_target_pairs={{0,1},{1,0},{2,3},{3,2},{4,5},{5,4},{6,7},{7,6},{8,9},{9,8},{10,11... | collective-permute-start | bytes 1351688 | tf_op jit(solution)/shard_map/ppermute | solution.py:390
  84.8 6.7 %collective-permute-start.1 = (f32[2,2,32,80]{3,2,1,0:T(8,128)S(1)}, f32[2,2,32,80]{3,2,1,0:T(8,128)S(1)}, u32[]{:S(2)}, u32[]{:S(2)}) collective-permute-start(f32[2,2,32,80]{3,2,1,0:T(8,128)S(1)} %direct_other.1), channel_id=1, source_target_pairs={{0,1},{1,0},{2,3},{3,2},{4,5},{5,4},{6,7},{7,6},{8,9},{9,8},{10,11... | collective-permute-start | bytes 122888 | tf_op jit(solution)/shard_map/ppermute | solution.py:472
